TPU v7x, 512 devices: a whole 4x8x8 slice. The times are simulated.
512 devices in a mesh: lat: 64 (over z_hi, y, core), wave: 8 (over x, z_lo).
Axes of the slice: x: 4, y: 8, z: 8 (z_hi: 4, z_lo: 2; z = z_hi * 2 + z_lo), core: 2. Of those that a mesh axis runs over, the one named last changes fastest.
Arguments:
- grid_field: float32 [16, 512, 768], P('wave', 'lat'), may hold values from -6 to 6
- row_longitudes: int32 [512], P('lat'), may hold values from 96 to 768, as said below
- owner_order: int32 [384], replicated, may hold values from 0 to 383, each once
- legendre: float32 [512, 384, 384], P('lat'), may hold values from -0.75 to 0.75
- vertical_band: float32 [4, 3, 4], replicated, may hold values from -1.5 to 1.5
Outputs:
- spectral: float32 [384, 384, 2, 16], P('lat', 'wave')
Inputs may be any that keep to these rules, and one draw needn't show every extreme that they name: `row_longitudes`: at least one row has all 768 longitudes. `owner_order`: each zonal wavenumber appears once; wave device g owns the slots g * 384 // 8 onward.
All inputs are finite; a program needn't handle non-finite values.
Results may differ from a plain program's by a relative error of at most 0.0003.
Values sent between devices are 32-bit elements; how exact they have to be, the bound alone decides.
A program may use at most 128 MiB of HBM per device.

v0:
```python
import math

import jax
import jax.numpy as jnp
from jax import lax
from jax.sharding import PartitionSpec as P

MW = 384
NLON = 768
FIELDS = 4
LEVELS = 4
NN = 384


def row_fourier(wavenumbers, row_values, row_points):
    columns = jnp.arange(NLON, dtype=jnp.int32)
    phase_steps = wavenumbers[None, :] * columns[:, None] % row_points
    phases = phase_steps.astype(jnp.float32) * (2.0 * math.pi / row_points.astype(jnp.float32))
    active = (columns[:, None] < row_points) & (2 * wavenumbers[None, :] < row_points)
    norm_factor = 1.0 / jnp.sqrt(row_points.astype(jnp.float32))
    cosine = jnp.where(active, jnp.cos(phases), 0.0) * norm_factor
    sine_part = jnp.where(active, -jnp.sin(phases), 0.0) * norm_factor
    transform = jnp.concatenate([cosine, sine_part], axis=1)
    return jnp.dot(
        row_values, transform, precision=lax.Precision.HIGHEST, preferred_element_type=jnp.float32
    )


def vertical(sums, vertical_band, degrees):
    components = sums.reshape(sums.shape[:3] + (FIELDS, LEVELS))
    sub_diagonal = vertical_band[:, 0, :]
    main_diagonal = vertical_band[:, 1, :]
    super_diagonal = vertical_band[:, 2, :]
    zero_level = jnp.zeros_like(components[..., :1])
    level_below = jnp.concatenate([zero_level, components[..., :-1]], axis=-1)
    level_above = jnp.concatenate([components[..., 1:], zero_level], axis=-1)
    coupled = sub_diagonal * level_below + main_diagonal * components + super_diagonal * level_above
    laplace_ratio = (degrees * (degrees + 1.0) / (MW * MW)).reshape(-1, 1, 1, 1, 1)
    return (components + laplace_ratio * coupled).reshape(sums.shape)


def shards(grid_field, row_longitudes, owner_order, legendre, vertical_band):
    local_layers, row_dev, longitudes = grid_field.shape
    wave_devices = lax.axis_size("wave")
    lat_devices = lax.axis_size("lat")
    group_waves = MW // wave_devices
    owned_degrees = NN // lat_devices

    def one_row(pair):
        return row_fourier(owner_order, pair[0], pair[1])

    fourier = lax.map(one_row, (jnp.moveaxis(grid_field, 1, 0), row_longitudes))
    fourier = fourier.reshape(row_dev, local_layers, 2, MW)
    owned = lax.all_to_all(fourier, "wave", split_axis=3, concat_axis=1, tiled=True)
    wave_index = lax.axis_index("wave")
    my_waves = lax.dynamic_slice_in_dim(owner_order, wave_index * group_waves, group_waves, 0)
    degree_ids = jnp.arange(NN, dtype=jnp.int32)
    triangle = degree_ids[None, :] >= my_waves[:, None]
    chosen = jnp.where(triangle[None], jnp.take(legendre, my_waves, axis=1), 0.0)
    sums = lax.psum_scatter(
        jnp.einsum("rkn,rlck->nkcl", chosen, owned, precision=lax.Precision.HIGHEST),
        "lat",
        scatter_dimension=0,
        tiled=True,
    )
    lat_index = lax.axis_index("lat")
    degrees = (lat_index * owned_degrees + jnp.arange(owned_degrees, dtype=jnp.int32)).astype(
        jnp.float32
    )
    return vertical(sums, vertical_band, degrees)


def solution(mesh):
    placed = (P("wave", "lat", None), P("lat"), P(), P("lat", None, None), P())
    return jax.shard_map(
        shards, mesh=mesh, in_specs=placed, out_specs=P("lat", "wave", None, None), check_vma=False
    )
```

profile of v0, /device:TPU:1, one launch (start us, length us, event | category | flops | bytes accessed | tf_op | source)
XLA Modules:
  0.0 386.5 jit_solution(15367746661120501559)
XLA Ops:
  7.4 181.0 %while.10 = (s32[]{:T(128)}, f32[8,2,768]{2,1,0:T(2,128)S(1)}, f32[8,2,768]{2,1,0:T(2,128)S(1)}, s32[8]{0:T(128)}, s32[384]{0:T(512)}, /*index=5*/s32[]{:T(128)}, f32[]{:T(128)}, s32[]{:T(128)}) while((s32[]{:T(128)}, f32[8,2,768]{2,1,0:T(2,128)S(1)}, f32[8,2,768]{2,1,0:T(2,128)S(1)}, s32[8]{0:T(128)}, s32[384]{0:T(512)}, ...), condition=%wide.region_1.2_spmd, body=%wide.region_0.1_spmd.sunk | while | flops 19465736 | bytes 4737457 | solution.py:52
  7.4 1.2 dynamic_slice.20
  9.7 1.2 multiply_compare_fusion.2
  12.2 16.6 %fusion.32 = (f32[768,384]{1,0:T(8,128)S(1)}, f32[768,384]{1,0:T(8,128)S(1)}) fusion(f32[]{:T(128)S(6)} %sqrt.4, f32[]{:T(128)S(6)} %div.10, s32[]{:T(128)S(6)} %select_n.63, s32[384]{0:T(512)} %get-tuple-element.107, pred[]{:T(512)S(6)} %lt.79, pred[384]{0:T(512)(128)(4,1)S(1)} %multiply_compare_fusion.2, pred[768]{0:T(1024)(128)(4,1)S(1)} %iota_compare_fusion.3), kind=kLoop, calls=%fused_computation.8.clone.1 | loop fusion | flops 4718592 | bytes 2361997 | tf_op jit(solution)/shard_map/while/body/eval_jaxpr/mul | solution.py:21
  30.0 1.2 dynamic_slice.20
  32.4 1.2 multiply_compare_fusion.2
  34.8 16.6 %fusion.32 = (f32[768,384]{1,0:T(8,128)S(1)}, f32[768,384]{1,0:T(8,128)S(1)}) fusion(f32[]{:T(128)S(6)} %sqrt.4, f32[]{:T(128)S(6)} %div.10, s32[]{:T(128)S(6)} %select_n.63, s32[384]{0:T(512)} %get-tuple-element.107, pred[]{:T(512)S(6)} %lt.79, pred[384]{0:T(512)(128)(4,1)S(1)} %multiply_compare_fusion.2, pred[768]{0:T(1024)(128)(4,1)S(1)} %iota_compare_fusion.3), kind=kLoop, calls=%fused_computation.8.clone.1 | loop fusion | flops 4718592 | bytes 2361997 | tf_op jit(solution)/shard_map/while/body/eval_jaxpr/mul | solution.py:21
  52.6 1.2 dynamic_slice.20
  55.0 1.2 multiply_compare_fusion.2
  57.4 16.6 %fusion.32 = (f32[768,384]{1,0:T(8,128)S(1)}, f32[768,384]{1,0:T(8,128)S(1)}) fusion(f32[]{:T(128)S(6)} %sqrt.4, f32[]{:T(128)S(6)} %div.10, s32[]{:T(128)S(6)} %select_n.63, s32[384]{0:T(512)} %get-tuple-element.107, pred[]{:T(512)S(6)} %lt.79, pred[384]{0:T(512)(128)(4,1)S(1)} %multiply_compare_fusion.2, pred[768]{0:T(1024)(128)(4,1)S(1)} %iota_compare_fusion.3), kind=kLoop, calls=%fused_computation.8.clone.1 | loop fusion | flops 4718592 | bytes 2361997 | tf_op jit(solution)/shard_map/while/body/eval_jaxpr/mul | solution.py:21
  75.2 1.2 dynamic_slice.20
  77.6 1.2 multiply_compare_fusion.2
  80.0 16.6 %fusion.32 = (f32[768,384]{1,0:T(8,128)S(1)}, f32[768,384]{1,0:T(8,128)S(1)}) fusion(f32[]{:T(128)S(6)} %sqrt.4, f32[]{:T(128)S(6)} %div.10, s32[]{:T(128)S(6)} %select_n.63, s32[384]{0:T(512)} %get-tuple-element.107, pred[]{:T(512)S(6)} %lt.79, pred[384]{0:T(512)(128)(4,1)S(1)} %multiply_compare_fusion.2, pred[768]{0:T(1024)(128)(4,1)S(1)} %iota_compare_fusion.3), kind=kLoop, calls=%fused_computation.8.clone.1 | loop fusion | flops 4718592 | bytes 2361997 | tf_op jit(solution)/shard_map/while/body/eval_jaxpr/mul | solution.py:21
  97.8 1.2 dynamic_slice.20
  100.2 1.2 multiply_compare_fusion.2
  102.7 16.6 %fusion.32 = (f32[768,384]{1,0:T(8,128)S(1)}, f32[768,384]{1,0:T(8,128)S(1)}) fusion(f32[]{:T(128)S(6)} %sqrt.4, f32[]{:T(128)S(6)} %div.10, s32[]{:T(128)S(6)} %select_n.63, s32[384]{0:T(512)} %get-tuple-element.107, pred[]{:T(512)S(6)} %lt.79, pred[384]{0:T(512)(128)(4,1)S(1)} %multiply_compare_fusion.2, pred[768]{0:T(1024)(128)(4,1)S(1)} %iota_compare_fusion.3), kind=kLoop, calls=%fused_computation.8.clone.1 | loop fusion | flops 4718592 | bytes 2361997 | tf_op jit(solution)/shard_map/while/body/eval_jaxpr/mul | solution.py:21
  120.4 1.2 dynamic_slice.20
  122.8 1.2 multiply_compare_fusion.2
  125.3 16.6 %fusion.32 = (f32[768,384]{1,0:T(8,128)S(1)}, f32[768,384]{1,0:T(8,128)S(1)}) fusion(f32[]{:T(128)S(6)} %sqrt.4, f32[]{:T(128)S(6)} %div.10, s32[]{:T(128)S(6)} %select_n.63, s32[384]{0:T(512)} %get-tuple-element.107, pred[]{:T(512)S(6)} %lt.79, pred[384]{0:T(512)(128)(4,1)S(1)} %multiply_compare_fusion.2, pred[768]{0:T(1024)(128)(4,1)S(1)} %iota_compare_fusion.3), kind=kLoop, calls=%fused_computation.8.clone.1 | loop fusion | flops 4718592 | bytes 2361997 | tf_op jit(solution)/shard_map/while/body/eval_jaxpr/mul | solution.py:21
  143.1 1.2 dynamic_slice.20
  145.4 1.2 multiply_compare_fusion.2
  147.9 16.6 %fusion.32 = (f32[768,384]{1,0:T(8,128)S(1)}, f32[768,384]{1,0:T(8,128)S(1)}) fusion(f32[]{:T(128)S(6)} %sqrt.4, f32[]{:T(128)S(6)} %div.10, s32[]{:T(128)S(6)} %select_n.63, s32[384]{0:T(512)} %get-tuple-element.107, pred[]{:T(512)S(6)} %lt.79, pred[384]{0:T(512)(128)(4,1)S(1)} %multiply_compare_fusion.2, pred[768]{0:T(1024)(128)(4,1)S(1)} %iota_compare_fusion.3), kind=kLoop, calls=%fused_computation.8.clone.1 | loop fusion | flops 4718592 | bytes 2361997 | tf_op jit(solution)/shard_map/while/body/eval_jaxpr/mul | solution.py:21
  165.7 1.2 dynamic_slice.20
  168.0 1.2 multiply_compare_fusion.2
  170.5 16.6 %fusion.32 = (f32[768,384]{1,0:T(8,128)S(1)}, f32[768,384]{1,0:T(8,128)S(1)}) fusion(f32[]{:T(128)S(6)} %sqrt.4, f32[]{:T(128)S(6)} %div.10, s32[]{:T(128)S(6)} %select_n.63, s32[384]{0:T(512)} %get-tuple-element.107, pred[]{:T(512)S(6)} %lt.79, pred[384]{0:T(512)(128)(4,1)S(1)} %multiply_compare_fusion.2, pred[768]{0:T(1024)(128)(4,1)S(1)} %iota_compare_fusion.3), kind=kLoop, calls=%fused_computation.8.clone.1 | loop fusion | flops 4718592 | bytes 2361997 | tf_op jit(solution)/shard_map/while/body/eval_jaxpr/mul | solution.py:21
  189.0 1.8 reshape.70
  190.9 6.7 %all-to-all-start = ((f32[8,1,1536]{2,1,0:T(1,128)}), f32[8,1,1536]{2,1,0:T(1,128)S(1)}, u32[]{:S(2)}, u32[]{:S(2)}) async-start(f32[8,1,1536]{2,1,0:T(1,128)} %reshape.70), calls=%async_computation | async-start | bytes 98304 | tf_op jit(solution)/shard_map/all_to_all | solution.py:54
  198.4 3.1 gather_fusion
  205.8 2.2 convolution_bitcast_fusion
  208.0 6.0 %copy.28 = f32[384,48,2,16]{1,3,2,0:T(8,128)} copy(f32[384,48,2,16]{0,3,2,1:T(8,128)S(1)} %convolution_bitcast_fusion) | data formatting | bytes 4718592 | tf_op jit(solution)/shard_map/rkn,rlck->nkcl/transpose | solution.py:61
  214.7 162.3 %reduce-scatter.2.cloned.1.call-done = f32[6,48,2,16]{1,3,2,0:T(8,128)} async-done(((f32[384,48,2,16]{1,3,2,0:T(8,128)}), f32[6,48,2,16]{1,3,2,0:T(8,128)}) %reduce-scatter.2.cloned.1.call-update) | async-done | bytes 36880 | tf_op jit(solution)/shard_map/reduce_scatter | solution.py:60
  378.0 1.7 multiply_add_fusion
  (38 shorter events, 22.5 us)
Async XLA Ops:
  190.9 11.8 %all-to-all-start = ((f32[8,1,1536]{2,1,0:T(1,128)}), f32[8,1,1536]{2,1,0:T(1,128)S(1)}, u32[]{:S(2)}, u32[]{:S(2)}) async-start(f32[8,1,1536]{2,1,0:T(1,128)} %reshape.70), calls=%async_computation | async-start | bytes 98304 | tf_op jit(solution)/shard_map/all_to_all | solution.py:54
  197.5 179.5 %reduce-scatter.2.cloned.1.call-start = ((), (), s32[]{:S(2)}) async-start(), calls=%async_computation.2 | async-start | bytes 6389760 | tf_op jit(solution)/shard_map/reduce_scatter | solution.py:60
  214.0 0.7 copy-start
Sparse Core Ops, SparseCore 0:
  214.2 162.7 reduce-scatter.1
where the time goes:
time: 392 us; the launch traced here: 386 us
  waiting for transfers between devices  163 us (42%)
  other arithmetic  150 us (38%)
  local copies, waits for them, and re-layouts  26.3 us (7%)
  loops' own time  14.4 us (4%)
  between operations  13.5 us (3%)
  matrix products  12 us (3%)
  starting transfers between devices  6.69 us (2%)
    reduce_scatter x1, waiting for transfers between devices, shards(): lax.psum_scatter(jnp.einsum('rkn,rlck->nkcl', chosen, owned, precision=la...  162 us
    mul x8, other arithmetic, row_fourier(): cosine = jnp.where(active, jnp.cos(phases), 0.0) * norm_factor  133 us
    another operation x1, loops' own time, shards(): fourier = lax.map(one_row, (jnp.moveaxis(grid_field, 1, 0), row_longitudes))  14.4 us
    lt x8, other arithmetic, row_fourier(): 2 * wavenumbers[None, :] < row_points  9.97 us
    dynamic_slice x8, local copies, waits for them, and re-layouts, shards(): fourier = lax.map(one_row, (jnp.moveaxis(grid_field, 1, 0), row_longitudes))  9.87 us
    dot_general x8, matrix products, row_fourier(): jnp.dot(row_values, transform, precision=lax.Precision.HIGHEST, preferred...  9.77 us
  transfers between devices with their start and end apart: 2, of which 2 were waited for; matrix products, arithmetic and copies ran while one was open for 1% of the time, Pallas kernels for 0%

commit v1 on v0

v1 whole, which is shorter than its diff:
```python
import functools

import jax
import jax.numpy as jnp
from jax import lax
from jax.experimental import pallas as pl
from jax.experimental.pallas import tpu as pltpu
from jax.sharding import PartitionSpec as P

MESH = pl.DeviceIdType.MESH
F32 = jnp.float32
BF16 = jnp.bfloat16

MW = 384
NN = 384
NLON = 768
FIELDS = 4
LEVELS = 4
LAYERS = 16
ZH = 4
NY = 8
NX = 4
ZL = 2
R = 8
KW = 48
NI = 6
NB = 128
NA = NLON // NB
JA = 8
JB = 4

COS = (1.0, -19.739208221435547, 64.93939208984375, -85.45665740966797, 60.242130279541016, -26.4046688079834,
       7.800131320953369, -1.4531123638153076)
SIN = (6.2831854820251465, -41.34170150756836, 81.6052474975586, -76.70580291748047, 42.05775451660156,
       -15.086565017700195, 3.7813189029693604, -0.6207788586616516)


def iota(shape, dim):
    return lax.broadcasted_iota(jnp.int32, shape, dim)


def split(x):
    hi = x.astype(BF16)
    return hi, (x - hi.astype(F32)).astype(BF16)


def nt(a, b):
    return lax.dot_general(a, b, (((1,), (1,)), ((), ())), preferred_element_type=F32)


def nn(a, b):
    return jnp.dot(a, b, preferred_element_type=F32)


def polynomial(coefficients, u):
    total = jnp.full_like(u, coefficients[-1])
    for c in coefficients[-2::-1]:
        total = total * u + c
    return total


def cos_sin(steps, points, inverse):
    turns = (steps - jnp.floor(steps * inverse + 0.5) * points) * inverse
    u = turns * turns
    return polynomial(COS, u), polynomial(SIN, u) * turns


def halves(extent):
    steps = []
    for s in range(extent // 2):
        for direction in (0, 1):
            for h in (0, 1):
                first = 0 if h == direction else 1
                if s >= first:
                    steps.append((direction, s, h, s > first))
    return steps


def kernel(
    grid_ref, lon_ref, order_ref, leg_ref, band_ref, out_ref,
    leg_v, gath, gx, e_s, tw_s, ft, xs, ra, rb, core_a, core_b, ring_a, ring_b, half_a, half_b,
    leg_sem, own_sem, g_send, g_recv, ca_send, ca_recv, cb_send, cb_recv,
    ra_send, ra_recv, rb_send, rb_recv, da_send, da_recv, db_send, db_recv,
):
    lw = LAYERS // (NX * ZL)
    lat, wave = lax.axis_index("lat"), lax.axis_index("wave")
    core = lax.rem(lat, 2)
    y = lax.rem(lat // 2, NY)
    zh = lat // (2 * NY)
    x = wave // ZL
    zl = lax.rem(wave, ZL)

    def at_y(o):
        return ((zh * NY + lax.rem(y + o + NY, NY)) * 2 + core, wave)

    def at_z(o):
        return ((lax.rem(zh + o + ZH, ZH) * NY + y) * 2 + core, wave)

    def at_w(dx, dz):
        return (lat, lax.rem(x + dx, NX) * ZL + lax.rem(zl + dz, ZL))

    sibling = (lat + 1 - 2 * core, wave)
    wave_peers = [(dx, dz) for dx in range(NX) for dz in range(ZL) if (dx, dz) != (0, 0)]

    leg_copies = []
    for t in range(NN // NB):
        copy = pltpu.make_async_copy(leg_ref.at[:, t * NB : (t + 1) * NB], leg_v.at[t], leg_sem.at[t])
        copy.start()
        leg_copies.append(copy)
    mine = pl.ds(pl.multiple_of(wave * (lw * R), 8), lw * R)
    own_copy = pltpu.make_async_copy(grid_ref, gath.at[mine], own_sem)
    own_copy.start()

    barrier = pltpu.get_barrier_semaphore()
    peers = [at_w(dx, dz) for dx, dz in wave_peers] + [sibling]
    peers += [at_y(o) for o in range(1, NY)] + [at_z(o) for o in range(1, ZH)]
    for peer in peers:
        pl.semaphore_signal(barrier, inc=1, device_id=peer, device_id_type=MESH)
    pl.semaphore_wait(barrier, len(peers))

    def remote(src, dst, send, recv, peer):
        copy = pltpu.make_async_remote_copy(
            src_ref=src, dst_ref=dst, send_sem=send, recv_sem=recv, device_id=peer, device_id_type=MESH
        )
        return copy

    grid_copies = []
    for i, (dx, dz) in enumerate(wave_peers):
        copy = remote(grid_ref, gath.at[mine], g_send.at[i], g_recv.at[i], at_w(dx, dz))
        copy.start()
        grid_copies.append(copy)

    sub = iota((8, NB), 0)
    waves = []
    for t in range(KW // 8):
        column = jnp.zeros((8, NB), F32)
        for s in range(8):
            column = jnp.where(sub == s, order_ref[wave * KW + t * 8 + s].astype(F32), column)
        waves.append(column)
    waves = jnp.concatenate(waves, axis=0)

    lane = iota((KW, NB), 1)
    low = lane.astype(F32)
    high = ((lane // LAYERS) * NB).astype(F32)
    for r in range(R):
        points = jnp.full((KW, NB), lon_ref[r], jnp.int32).astype(F32)
        inverse = 1.0 / points
        cos_low, sin_low = cos_sin(waves * low, points, inverse)
        table_hi, table_lo = split(jnp.concatenate([cos_low, -sin_low], axis=0))
        e_s[r * 2 * KW : (r + 1) * 2 * KW, :] = jnp.concatenate([table_hi, table_hi, table_lo], axis=1)
        cos_high, sin_high = cos_sin(waves * high, points, inverse)
        factor = jnp.where(2.0 * waves < points, 1.0 / jnp.sqrt(points), 0.0)
        tw_s[r * 2 * KW : r * 2 * KW + KW, :] = cos_high * factor
        tw_s[r * 2 * KW + KW : (r + 1) * 2 * KW, :] = -sin_high * factor

    n_lane = iota((1, NN), 1).astype(F32) + 0.5
    z_of = jnp.floor(n_lane * (1.0 / (NI * 2 * NY)))
    rest = n_lane - z_of * (NI * 2 * NY)
    y_of = jnp.floor(rest * (1.0 / (NI * 2)))
    rest = rest - y_of * (NI * 2)
    c_of = jnp.floor(rest * (1.0 / NI))
    i_of = rest - c_of * NI - 0.5
    z_rel = z_of - zh.astype(F32)
    z_rel = jnp.where(z_rel < 0, z_rel + ZH, z_rel)
    y_rel = y_of - y.astype(F32)
    y_rel = jnp.where(y_rel < 0, y_rel + NY, y_rel)
    c_rel = jnp.where(c_of == core.astype(F32), 0.0, 1.0)
    n_row = iota((NN, NN), 0).astype(F32)
    place_a = ((c_rel * NY + y_rel) * ZH + z_rel) * NI + i_of
    place_b = ((c_rel * ZH + z_rel) * NY + y_rel) * NI + i_of
    order_a = jnp.where(n_row == place_a, 1.0, 0.0).astype(BF16)
    order_b = jnp.where(n_row == place_b, 1.0, 0.0).astype(BF16)

    def slot(g, q):
        return (q % 4) * (KW // 4) + 2 * g + q // 4

    groups = KW // 8
    for copy in leg_copies:
        copy.wait()
    n_of = iota((R, NN), 1)
    for g in range(groups):
        rows = []
        for q in range(8):
            m = order_ref[wave * KW + slot(g, q)]
            picked = jnp.concatenate([leg_v[t, pl.ds(m, R, stride=MW), :] for t in range(NN // NB)], axis=1)
            rows.append(jnp.where(n_of >= m, picked, 0.0))
        hi, lo = split(jnp.concatenate(rows, axis=0))
        turned = nt(order_a if 2 * g < JA else order_b, jnp.concatenate([hi, lo], axis=0))
        xs[g] = turned.astype(BF16)

    own_copy.wait()
    for copy in grid_copies:
        copy.wait_recv()
    for layer in range(LAYERS):
        for a in range(NA):
            gx[a, pl.ds(layer, R, stride=LAYERS), :] = gath[layer * R : (layer + 1) * R, a * NB : (a + 1) * NB]

    spread = jnp.where(iota((2 * NB, NB), 0) % LAYERS == iota((2 * NB, NB), 1) % LAYERS, 1.0, 0.0).astype(BF16)
    column = iota((LAYERS, NB), 1)
    for r in range(R):
        points = lon_ref[r]
        parts = [
            jnp.where(column + a * NB < points, gx[a, r * LAYERS : (r + 1) * LAYERS, :], 0.0) for a in range(NA)
        ]
        parts += [jnp.zeros((LAYERS, NB), F32)] * (NB // LAYERS - NA)
        hi, lo = split(jnp.concatenate(parts, axis=0))
        first = nt(e_s[r * 2 * KW : (r + 1) * 2 * KW, :], jnp.concatenate([hi, lo, hi], axis=1))
        re, im = first[:KW], first[KW:]
        tw_re = tw_s[r * 2 * KW : r * 2 * KW + KW, :]
        tw_im = tw_s[r * 2 * KW + KW : (r + 1) * 2 * KW, :]
        both = jnp.concatenate([re * tw_re - im * tw_im, re * tw_im + im * tw_re], axis=0)
        hi, lo = split(both)
        ft[r * 2 * KW : (r + 1) * 2 * KW, :] = nn(jnp.concatenate([hi, lo], axis=1), spread)

    lanes = iota((R, NB), 1)
    k4_of = lanes // (2 * LAYERS)
    is_cos = (lanes // LAYERS) % 2 == 0
    diagonals = []
    for g in range(groups):
        rows = []
        for q in range(8):
            k = slot(g, q)
            value = jnp.where(is_cos, ft[pl.ds(k, R, stride=2 * KW), :], ft[pl.ds(KW + k, R, stride=2 * KW), :])
            value = jnp.where(k4_of == q % 4, value, 0.0)
            zero = jnp.zeros((R, NB), F32)
            rows.append(jnp.concatenate([value, zero] if q < 4 else [zero, value], axis=1))
        hi, lo = split(jnp.concatenate(rows, axis=0))
        diagonals.append(jnp.concatenate([hi, hi, lo, lo], axis=0))

    half_n = NN // 2

    def partial_sums(c):
        for g in range(groups):
            turned = xs[g, c * half_n : (c + 1) * half_n, :]
            sums = nn(jnp.concatenate([turned, turned], axis=1), diagonals[g])
            for t in (0, 1):
                j = 2 * g + t
                value = sums[:, t * NB : (t + 1) * NB]
                if j < JA:
                    ra[pl.ds(c * half_n * JA + j, half_n, stride=JA), :] = value
                else:
                    rb[pl.ds(c * half_n * JB + j - JA, half_n, stride=JB), :] = value

    part_a = ZH * NI * JA
    part_b = NY * NI * JB
    y_order = sorted(range(NY), key=lambda o: -min(o, NY - o))
    z_order = sorted(range(ZH), key=lambda o: -min(o, ZH - o))

    partial_sums(1)
    core_copies = []
    copies_a, copies_b = {}, {}
    for at in range(max(NY, ZH)):
        if at < NY:
            o = y_order[at]
            copies_a[o] = remote(
                ra.at[pl.ds(half_n * JA + o * part_a, part_a)], core_a.at[pl.ds(o * part_a, part_a)],
                ca_send.at[o], ca_recv.at[o], sibling,
            )
            copies_a[o].start()
        if at < ZH:
            o = z_order[at]
            copies_b[o] = remote(
                rb.at[pl.ds(half_n * JB + o * part_b, part_b)], core_b.at[pl.ds(o * part_b, part_b)],
                cb_send.at[o], cb_recv.at[o], sibling,
            )
            copies_b[o].start()
    partial_sums(0)

    ha, hb = part_a // 2, part_b // 2
    started = []
    done_a, done_b = set(), set()

    def own_part(o, own, from_core, copies, done, part):
        if o not in done:
            copies[o].wait_recv()
            done.add(o)
            rows = pl.ds(o * part, part)
            own[rows, :] = own[rows, :] + from_core[rows, :]

    def ring_step(item, extent, own, from_core, copies, done, part, ring, send, recv, at, pending):
        direction, s, h, has = item
        o = extent // 2 - s if direction == 0 else extent // 2 + s
        own_part(o, own, from_core, copies, done, part)
        rows = pl.ds(o * part + h * (part // 2), part // 2)
        if has:
            pending[(direction, s - 1, h)].wait_recv()
            own[rows, :] = own[rows, :] + ring[direction, s - 1, h]
        copy = remote(
            own.at[rows], ring.at[direction, s, h], send.at[direction, s, h], recv.at[direction, s, h],
            at(1 if direction == 0 else -1),
        )
        copy.start()
        pending[(direction, s, h)] = copy

    def ring_end(extent, own, from_core, copies, done, part, ring, pending, h):
        own_part(0, own, from_core, copies, done, part)
        rows = pl.ds(h * (part // 2), part // 2)
        total = own[rows, :]
        for direction in (0, 1):
            last = (direction, extent // 2 - 1, h)
            if last in pending:
                pending[last].wait_recv()
                total = total + ring[direction, extent // 2 - 1, h]
        own[rows, :] = total

    pend_a, pend_b = {}, {}
    args_a = (NY, ra, core_a, copies_a, done_a, part_a, ring_a)
    args_b = (ZH, rb, core_b, copies_b, done_b, part_b, ring_b)
    for s in range(max(NY, ZH) // 2):
        for item in halves(NY):
            if item[1] == s:
                ring_step(item, *args_a, ra_send, ra_recv, at_y, pend_a)
        for item in halves(ZH):
            if item[1] == s:
                ring_step(item, *args_b, rb_send, rb_recv, at_z, pend_b)

    for h in (0, 1):
        ring_end(*args_b, pend_b, h)
    rows_b = NI * JB
    direct_b = []
    for o in range(1, NY):
        copy = remote(
            rb.at[pl.ds(o * rows_b, rows_b)], half_b.at[pl.ds((o - 1) * rows_b, rows_b)],
            db_send.at[o - 1], db_recv.at[o - 1], at_y(o),
        )
        copy.start()
        direct_b.append(copy)
    for h in (0, 1):
        ring_end(*args_a, pend_a, h)
    rows_a = NI * JA
    direct_a = []
    for o in range(1, ZH):
        copy = remote(
            ra.at[pl.ds(o * rows_a, rows_a)], half_a.at[pl.ds((o - 1) * rows_a, rows_a)],
            da_send.at[o - 1], da_recv.at[o - 1], at_z(o),
        )
        copy.start()
        direct_a.append(copy)

    band = [jnp.zeros((1, NB), F32) for _ in range(3)]
    layer_of = iota((1, NB), 1) % LAYERS
    for d in range(3):
        for f in range(FIELDS):
            for l in range(LEVELS):
                if (d, l) in ((0, 0), (2, LEVELS - 1)):
                    continue
                band[d] = jnp.where(layer_of == f * LEVELS + l, band_ref[d, f, l], band[d])

    def vertical(total, width):
        degree = iota(total.shape, 0) // width + lat * NI
        degree = degree.astype(F32)
        ratio = degree * (degree + 1.0) * (1.0 / (MW * MW))
        below = pltpu.roll(total, 1, 1)
        above = pltpu.roll(total, NB - 1, 1)
        return total + ratio * (band[0] * below + band[1] * total + band[2] * above)

    total_b = rb[:rows_b, :]
    for o in range(1, NY):
        direct_b[o - 1].wait_recv()
        total_b = total_b + half_b[(o - 1) * rows_b : o * rows_b, :]
    total_b = vertical(total_b, JB)
    total_a = ra[:rows_a, :]
    for o in range(1, ZH):
        direct_a[o - 1].wait_recv()
        total_a = total_a + half_a[(o - 1) * rows_a : o * rows_a, :]
    total_a = vertical(total_a, JA)

    fill = jnp.zeros((NB - rows_a - rows_b, NB), F32)
    turned = jnp.concatenate([total_a, total_b, fill], axis=0).T
    cl = 2 * LAYERS
    for i in range(NI):
        pieces = []
        for k4 in range(4):
            rows = turned[k4 * cl : (k4 + 1) * cl]
            pieces.append(rows[:, i * JA : (i + 1) * JA])
            pieces.append(rows[:, rows_a + i * JB : rows_a + (i + 1) * JB])
        out_ref[i] = jnp.concatenate(pieces, axis=1)

    sent = grid_copies + list(copies_a.values()) + list(copies_b.values()) + list(pend_a.values())
    for copy in sent + list(pend_b.values()) + direct_a + direct_b:
        copy.wait_send()


def shards(grid_field, row_longitudes, owner_order, legendre, vertical_band):
    lw = grid_field.shape[0]
    dma = pltpu.SemaphoreType.DMA
    vmem = pltpu.VMEM
    smem = pl.BlockSpec(memory_space=pltpu.SMEM)
    hbm = pl.BlockSpec(memory_space=pltpu.HBM)
    part_a, part_b = ZH * NI * JA, NY * NI * JB
    out = pl.pallas_call(
        kernel,
        out_shape=jax.ShapeDtypeStruct((NI, 2 * LAYERS, KW), F32),
        in_specs=[hbm, smem, smem, hbm, smem],
        out_specs=pl.BlockSpec(memory_space=pltpu.VMEM),
        scratch_shapes=[
            vmem((NN // NB, R * MW, NB), F32),
            vmem((LAYERS * R, NLON), F32),
            vmem((NA, R * LAYERS, NB), F32),
            vmem((R * 2 * KW, 3 * NB), BF16),
            vmem((R * 2 * KW, NB), F32),
            vmem((R * 2 * KW, NB), F32),
            vmem((KW // 8, NN, NB), BF16),
            vmem((NN * JA, NB), F32),
            vmem((NN * JB, NB), F32),
            vmem((NN // 2 * JA, NB), F32),
            vmem((NN // 2 * JB, NB), F32),
            vmem((2, NY // 2, 2, part_a // 2, NB), F32),
            vmem((2, ZH // 2, 2, part_b // 2, NB), F32),
            vmem(((ZH - 1) * NI * JA, NB), F32),
            vmem(((NY - 1) * NI * JB, NB), F32),
            dma((NN // NB,)), dma,
            dma((NX * ZL - 1,)), dma((NX * ZL - 1,)),
            dma((NY,)), dma((NY,)), dma((ZH,)), dma((ZH,)),
            dma((2, NY // 2, 2)), dma((2, NY // 2, 2)), dma((2, ZH // 2, 2)), dma((2, ZH // 2, 2)),
            dma((ZH - 1,)), dma((ZH - 1,)), dma((NY - 1,)), dma((NY - 1,)),
        ],
        compiler_params=pltpu.CompilerParams(
            collective_id=0, has_side_effects=True, vmem_limit_bytes=60 * 1024 * 1024
        ),
    )(
        grid_field.reshape(lw * R, NLON), row_longitudes, owner_order, legendre.reshape(R * MW, NN),
        vertical_band.transpose(1, 0, 2),
    )
    return out.reshape(NI, 2, LAYERS, KW).transpose(0, 3, 1, 2)


def solution(mesh):
    placed = (P("wave", "lat", None), P("lat"), P(), P("lat", None, None), P())
    return jax.shard_map(
        shards, mesh=mesh, in_specs=placed, out_specs=P("lat", "wave", None, None), check_vma=False
    )
```

time: 392 us -> 47.9 us (0.12)
  the two profiles are of different devices: /device:TPU:1 before, /device:TPU:2 now
where the time goes in v1:
time: 47.9 us; the launch traced here: 47.7 us
  Pallas kernels  46.2 us (96%)
  local copies, waits for them, and re-layouts  1.54 us (3%)
    pallas_call x1, Pallas kernels, shards(): pl.pallas_call(kernel, out_shape=jax.ShapeDtypeStruct((NI, 2 * LAYERS, KW...  46.2 us
    unnamed x1, local copies, waits for them, and re-layouts  1.54 us

profile of v1, /device:TPU:2, one launch (start us, length us, event | category | flops | bytes accessed | tf_op | source)
XLA Modules:
  0.0 47.7 jit_solution(11714099949240099008)
XLA Ops:
  0.0 46.2 %shard_map.55 = f32[6,32,48]{2,1,0:T(8,128)} custom-call(f32[16,768]{1,0:T(8,128)} %bitcast.8, s32[8]{0:T(128)} %lon_ref.1, s32[384]{0:T(512)} %order_ref.1, f32[3072,384]{1,0:T(8,128)} %bitcast.6, f32[3,4,4]{2,1,0:T(4,128)} %bitcast.9), custom_call_target="tpu_custom_call" | custom-call | tf_op jit(solution)/shard_map/pallas_call | solution.py:391
  46.2 1.5 %copy.7 = f32[6,48,2,16]{1,3,2,0:T(8,128)} copy(f32[6,48,2,16]{1,3,2,0:T(8,128)} %bitcast.7) | data formatting | bytes 73728

commit v2 on v1

--- a/solution.py
+++ b/solution.py
@@ -78,7 +78,7 @@
 
 def kernel(
     grid_ref, lon_ref, order_ref, leg_ref, band_ref, out_ref,
-    leg_v, gath, gx, e_s, tw_s, ft, xs, ra, rb, core_a, core_b, ring_a, ring_b, half_a, half_b,
+    leg_v, gath, gx, e_s, tw_s, ft, xs, ra, rb, core_a, core_b, ring_a, far_b, half_a, half_b,
     leg_sem, own_sem, g_send, g_recv, ca_send, ca_recv, cb_send, cb_recv,
     ra_send, ra_recv, rb_send, rb_recv, da_send, da_recv, db_send, db_recv,
 ):
@@ -90,11 +90,11 @@
     x = wave // ZL
     zl = lax.rem(wave, ZL)
 
-    def at_y(o):
-        return ((zh * NY + lax.rem(y + o + NY, NY)) * 2 + core, wave)
-
-    def at_z(o):
-        return ((lax.rem(zh + o + ZH, ZH) * NY + y) * 2 + core, wave)
+    def at_y(o, c):
+        return ((zh * NY + lax.rem(y + o + NY, NY)) * 2 + c, wave)
+
+    def at_z(o, c):
+        return ((lax.rem(zh + o + ZH, ZH) * NY + y) * 2 + c, wave)
 
     def at_w(dx, dz):
         return (lat, lax.rem(x + dx, NX) * ZL + lax.rem(zl + dz, ZL))
@@ -112,17 +112,29 @@
     own_copy.start()
 
     barrier = pltpu.get_barrier_semaphore()
-    peers = [at_w(dx, dz) for dx, dz in wave_peers] + [sibling]
-    peers += [at_y(o) for o in range(1, NY)] + [at_z(o) for o in range(1, ZH)]
-    for peer in peers:
-        pl.semaphore_signal(barrier, inc=1, device_id=peer, device_id_type=MESH)
-    pl.semaphore_wait(barrier, len(peers))
+    both = [at_w(dx, dz) for dx, dz in wave_peers] + [sibling]
+
+    def enter(others, expected):
+        for peer in both + others:
+            pl.semaphore_signal(barrier, inc=1, device_id=peer, device_id_type=MESH)
+        pl.semaphore_wait(barrier, len(both) + expected)
+
+    z_far, y_far = range(1, ZH), range(1, NY)
+
+    @pl.when(core == 1)
+    def _():
+        others = [at_y(1, 1), at_y(-1, 1)] + [at_z(o, 1) for o in z_far] + [at_y(o, 0) for o in y_far]
+        enter(others, 2 + 2 * (ZH - 1))
+
+    @pl.when(core == 0)
+    def _():
+        others = [at_z(o, 1) for o in z_far] + [at_z(o, 0) for o in z_far] + [at_y(o, 0) for o in y_far]
+        enter(others, ZH - 1 + 2 * (NY - 1))
 
     def remote(src, dst, send, recv, peer):
-        copy = pltpu.make_async_remote_copy(
+        return pltpu.make_async_remote_copy(
             src_ref=src, dst_ref=dst, send_sem=send, recv_sem=recv, device_id=peer, device_id_type=MESH
         )
-        return copy
 
     grid_copies = []
     for i, (dx, dz) in enumerate(wave_peers):
@@ -164,10 +176,9 @@
     z_rel = jnp.where(z_rel < 0, z_rel + ZH, z_rel)
     y_rel = y_of - y.astype(F32)
     y_rel = jnp.where(y_rel < 0, y_rel + NY, y_rel)
-    c_rel = jnp.where(c_of == core.astype(F32), 0.0, 1.0)
     n_row = iota((NN, NN), 0).astype(F32)
-    place_a = ((c_rel * NY + y_rel) * ZH + z_rel) * NI + i_of
-    place_b = ((c_rel * ZH + z_rel) * NY + y_rel) * NI + i_of
+    place_a = ((y_rel * ZH + z_rel) * 2 + c_of) * NI + i_of
+    place_b = ((z_rel * NY + y_rel) * 2 + c_of) * NI + i_of
     order_a = jnp.where(n_row == place_a, 1.0, 0.0).astype(BF16)
     order_b = jnp.where(n_row == place_b, 1.0, 0.0).astype(BF16)
 
@@ -227,115 +238,121 @@
         hi, lo = split(jnp.concatenate(rows, axis=0))
         diagonals.append(jnp.concatenate([hi, hi, lo, lo], axis=0))
 
-    half_n = NN // 2
-
-    def partial_sums(c):
-        for g in range(groups):
-            turned = xs[g, c * half_n : (c + 1) * half_n, :]
+    def partial_sums(first, last):
+        for g in range(first, last):
+            turned = xs[g]
             sums = nn(jnp.concatenate([turned, turned], axis=1), diagonals[g])
             for t in (0, 1):
                 j = 2 * g + t
                 value = sums[:, t * NB : (t + 1) * NB]
                 if j < JA:
-                    ra[pl.ds(c * half_n * JA + j, half_n, stride=JA), :] = value
+                    ra[pl.ds(j, NN, stride=JA), :] = value
                 else:
-                    rb[pl.ds(c * half_n * JB + j - JA, half_n, stride=JB), :] = value
-
-    part_a = ZH * NI * JA
-    part_b = NY * NI * JB
+                    rb[pl.ds(j - JA, NN, stride=JB), :] = value
+
+    part_a = NN // NY * JA
+    part_b = NN // ZH * JB
+    rows_a, rows_b = NI * JA, NI * JB
     y_order = sorted(range(NY), key=lambda o: -min(o, NY - o))
     z_order = sorted(range(ZH), key=lambda o: -min(o, ZH - o))
-
-    partial_sums(1)
-    core_copies = []
-    copies_a, copies_b = {}, {}
-    for at in range(max(NY, ZH)):
-        if at < NY:
-            o = y_order[at]
-            copies_a[o] = remote(
-                ra.at[pl.ds(half_n * JA + o * part_a, part_a)], core_a.at[pl.ds(o * part_a, part_a)],
-                ca_send.at[o], ca_recv.at[o], sibling,
-            )
-            copies_a[o].start()
-        if at < ZH:
-            o = z_order[at]
-            copies_b[o] = remote(
-                rb.at[pl.ds(half_n * JB + o * part_b, part_b)], core_b.at[pl.ds(o * part_b, part_b)],
-                cb_send.at[o], cb_recv.at[o], sibling,
-            )
-            copies_b[o].start()
-    partial_sums(0)
-
-    ha, hb = part_a // 2, part_b // 2
-    started = []
-    done_a, done_b = set(), set()
-
-    def own_part(o, own, from_core, copies, done, part):
-        if o not in done:
-            copies[o].wait_recv()
-            done.add(o)
-            rows = pl.ds(o * part, part)
-            own[rows, :] = own[rows, :] + from_core[rows, :]
-
-    def ring_step(item, extent, own, from_core, copies, done, part, ring, send, recv, at, pending):
-        direction, s, h, has = item
-        o = extent // 2 - s if direction == 0 else extent // 2 + s
-        own_part(o, own, from_core, copies, done, part)
-        rows = pl.ds(o * part + h * (part // 2), part // 2)
-        if has:
-            pending[(direction, s - 1, h)].wait_recv()
-            own[rows, :] = own[rows, :] + ring[direction, s - 1, h]
-        copy = remote(
-            own.at[rows], ring.at[direction, s, h], send.at[direction, s, h], recv.at[direction, s, h],
-            at(1 if direction == 0 else -1),
+    cut = JA // 2
+
+    def core_a_copy(o):
+        rows = pl.ds(o * part_a, part_a)
+        return remote(ra.at[rows], core_a.at[rows], ca_send.at[o], ca_recv.at[o], sibling)
+
+    def core_b_copy(o):
+        rows = pl.ds(o * part_b, part_b)
+        return remote(rb.at[rows], core_b.at[rows], cb_send.at[o], cb_recv.at[o], sibling)
+
+    def ring_copy(direction, s, h):
+        o = NY // 2 - s if direction == 0 else NY // 2 + s
+        rows = pl.ds(o * part_a + h * (part_a // 2), part_a // 2)
+        return remote(
+            ra.at[rows], ring_a.at[direction, s, h], ra_send.at[direction, s, h], ra_recv.at[direction, s, h],
+            at_y(1 if direction == 0 else -1, 1),
         )
-        copy.start()
-        pending[(direction, s, h)] = copy
-
-    def ring_end(extent, own, from_core, copies, done, part, ring, pending, h):
-        own_part(0, own, from_core, copies, done, part)
-        rows = pl.ds(h * (part // 2), part // 2)
-        total = own[rows, :]
-        for direction in (0, 1):
-            last = (direction, extent // 2 - 1, h)
-            if last in pending:
-                pending[last].wait_recv()
-                total = total + ring[direction, extent // 2 - 1, h]
-        own[rows, :] = total
-
-    pend_a, pend_b = {}, {}
-    args_a = (NY, ra, core_a, copies_a, done_a, part_a, ring_a)
-    args_b = (ZH, rb, core_b, copies_b, done_b, part_b, ring_b)
-    for s in range(max(NY, ZH) // 2):
-        for item in halves(NY):
-            if item[1] == s:
-                ring_step(item, *args_a, ra_send, ra_recv, at_y, pend_a)
-        for item in halves(ZH):
-            if item[1] == s:
-                ring_step(item, *args_b, rb_send, rb_recv, at_z, pend_b)
-
-    for h in (0, 1):
-        ring_end(*args_b, pend_b, h)
-    rows_b = NI * JB
-    direct_b = []
-    for o in range(1, NY):
-        copy = remote(
-            rb.at[pl.ds(o * rows_b, rows_b)], half_b.at[pl.ds((o - 1) * rows_b, rows_b)],
-            db_send.at[o - 1], db_recv.at[o - 1], at_y(o),
+
+    def far_copy(o):
+        return remote(
+            rb.at[pl.ds(o * part_b, part_b)], far_b.at[pl.ds((o - 1) * part_b, part_b)],
+            rb_send.at[o - 1], rb_recv.at[o - 1], at_z(o, 0),
         )
-        copy.start()
-        direct_b.append(copy)
-    for h in (0, 1):
-        ring_end(*args_a, pend_a, h)
-    rows_a = NI * JA
-    direct_a = []
-    for o in range(1, ZH):
-        copy = remote(
-            ra.at[pl.ds(o * rows_a, rows_a)], half_a.at[pl.ds((o - 1) * rows_a, rows_a)],
-            da_send.at[o - 1], da_recv.at[o - 1], at_z(o),
+
+    def end_a_copy(o, c):
+        return remote(
+            ra.at[pl.ds((o * 2 + c) * rows_a, rows_a)], half_a.at[pl.ds(o * rows_a, rows_a)],
+            da_send.at[o, c], da_recv.at[o], at_z(o, c) if o else sibling,
         )
-        copy.start()
-        direct_a.append(copy)
+
+    def end_b_copy(o, c):
+        return remote(
+            rb.at[pl.ds((o * 2 + c) * rows_b, rows_b)], half_b.at[pl.ds(o * rows_b, rows_b)],
+            db_send.at[o, c], db_recv.at[o], at_y(o, c) if o else sibling,
+        )
+
+    end_a = [(o, c) for o in z_order for c in (0, 1) if (o, c) != (0, 1)]
+    end_b = [(o, c) for o in y_order for c in (0, 1) if (o, c) != (0, 0)]
+
+    @pl.when(core == 1)
+    def _():
+        partial_sums(cut, groups)
+        for o in z_order:
+            core_b_copy(o).start()
+        partial_sums(0, cut)
+        seen = set()
+
+        def own_part(o):
+            if o not in seen:
+                seen.add(o)
+                core_a_copy(o).wait_recv()
+                rows = pl.ds(o * part_a, part_a)
+                ra[rows, :] = ra[rows, :] + core_a[rows, :]
+
+        for direction, s, h, has in halves(NY):
+            o = NY // 2 - s if direction == 0 else NY // 2 + s
+            own_part(o)
+            if has:
+                rows = pl.ds(o * part_a + h * (part_a // 2), part_a // 2)
+                ring_copy(direction, s - 1, h).wait_recv()
+                ra[rows, :] = ra[rows, :] + ring_a[direction, s - 1, h]
+            ring_copy(direction, s, h).start()
+        own_part(0)
+        last = NY // 2 - 1
+        for h in (0, 1):
+            rows = pl.ds(h * (part_a // 2), part_a // 2)
+            total = ra[rows, :]
+            for direction in (0, 1):
+                if (direction, last, h) in [item[:3] for item in halves(NY)]:
+                    ring_copy(direction, last, h).wait_recv()
+                    total = total + ring_a[direction, last, h]
+            ra[rows, :] = total
+        for o, c in end_a:
+            end_a_copy(o, c).start()
+        half_a[:rows_a, :] = ra[rows_a : 2 * rows_a, :]
+        end_b_copy(0, 1).wait_recv()
+
+    @pl.when(core == 0)
+    def _():
+        partial_sums(0, cut)
+        for o in y_order:
+            core_a_copy(o).start()
+        partial_sums(cut, groups)
+        for o in z_order:
+            core_b_copy(o).wait_recv()
+            rows = pl.ds(o * part_b, part_b)
+            rb[rows, :] = rb[rows, :] + core_b[rows, :]
+            if o:
+                far_copy(o).start()
+        total = rb[:part_b, :]
+        for o in z_far:
+            far_copy(o).wait_recv()
+            total = total + far_b[(o - 1) * part_b : o * part_b, :]
+        rb[:part_b, :] = total
+        for o, c in end_b:
+            end_b_copy(o, c).start()
+        half_b[:rows_b, :] = rb[:rows_b, :]
+        end_a_copy(0, 0).wait_recv()
 
     band = [jnp.zeros((1, NB), F32) for _ in range(3)]
     layer_of = iota((1, NB), 1) % LAYERS
@@ -354,15 +371,15 @@
         above = pltpu.roll(total, NB - 1, 1)
         return total + ratio * (band[0] * below + band[1] * total + band[2] * above)
 
-    total_b = rb[:rows_b, :]
-    for o in range(1, NY):
-        direct_b[o - 1].wait_recv()
-        total_b = total_b + half_b[(o - 1) * rows_b : o * rows_b, :]
+    total_b = half_b[:rows_b, :]
+    for o in y_far:
+        end_b_copy(o, 0).wait_recv()
+        total_b = total_b + half_b[o * rows_b : (o + 1) * rows_b, :]
     total_b = vertical(total_b, JB)
-    total_a = ra[:rows_a, :]
-    for o in range(1, ZH):
-        direct_a[o - 1].wait_recv()
-        total_a = total_a + half_a[(o - 1) * rows_a : o * rows_a, :]
+    total_a = half_a[:rows_a, :]
+    for o in z_far:
+        end_a_copy(o, 0).wait_recv()
+        total_a = total_a + half_a[o * rows_a : (o + 1) * rows_a, :]
     total_a = vertical(total_a, JA)
 
     fill = jnp.zeros((NB - rows_a - rows_b, NB), F32)
@@ -376,9 +393,26 @@
             pieces.append(rows[:, rows_a + i * JB : rows_a + (i + 1) * JB])
         out_ref[i] = jnp.concatenate(pieces, axis=1)
 
-    sent = grid_copies + list(copies_a.values()) + list(copies_b.values()) + list(pend_a.values())
-    for copy in sent + list(pend_b.values()) + direct_a + direct_b:
+    for copy in grid_copies:
         copy.wait_send()
+
+    @pl.when(core == 1)
+    def _():
+        for o in z_order:
+            core_b_copy(o).wait_send()
+        for direction, s, h, _ in halves(NY):
+            ring_copy(direction, s, h).wait_send()
+        for o, c in end_a:
+            end_a_copy(o, c).wait_send()
+
+    @pl.when(core == 0)
+    def _():
+        for o in y_order:
+            core_a_copy(o).wait_send()
+        for o in z_far:
+            far_copy(o).wait_send()
+        for o, c in end_b:
+            end_b_copy(o, c).wait_send()
 
 
 def shards(grid_field, row_longitudes, owner_order, legendre, vertical_band):
@@ -387,7 +421,7 @@
     vmem = pltpu.VMEM
     smem = pl.BlockSpec(memory_space=pltpu.SMEM)
     hbm = pl.BlockSpec(memory_space=pltpu.HBM)
-    part_a, part_b = ZH * NI * JA, NY * NI * JB
+    part_a, part_b = NN // NY * JA, NN // ZH * JB
     out = pl.pallas_call(
         kernel,
         out_shape=jax.ShapeDtypeStruct((NI, 2 * LAYERS, KW), F32),
@@ -403,17 +437,17 @@
             vmem((KW // 8, NN, NB), BF16),
             vmem((NN * JA, NB), F32),
             vmem((NN * JB, NB), F32),
-            vmem((NN // 2 * JA, NB), F32),
-            vmem((NN // 2 * JB, NB), F32),
+            vmem((NN * JA, NB), F32),
+            vmem((NN * JB, NB), F32),
             vmem((2, NY // 2, 2, part_a // 2, NB), F32),
-            vmem((2, ZH // 2, 2, part_b // 2, NB), F32),
-            vmem(((ZH - 1) * NI * JA, NB), F32),
-            vmem(((NY - 1) * NI * JB, NB), F32),
+            vmem(((ZH - 1) * part_b, NB), F32),
+            vmem((ZH * NI * JA, NB), F32),
+            vmem((NY * NI * JB, NB), F32),
             dma((NN // NB,)), dma,
             dma((NX * ZL - 1,)), dma((NX * ZL - 1,)),
             dma((NY,)), dma((NY,)), dma((ZH,)), dma((ZH,)),
-            dma((2, NY // 2, 2)), dma((2, NY // 2, 2)), dma((2, ZH // 2, 2)), dma((2, ZH // 2, 2)),
-            dma((ZH - 1,)), dma((ZH - 1,)), dma((NY - 1,)), dma((NY - 1,)),
+            dma((2, NY // 2, 2)), dma((2, NY // 2, 2)), dma((ZH - 1,)), dma((ZH - 1,)),
+            dma((ZH, 2)), dma((ZH,)), dma((NY, 2)), dma((NY,)),
         ],
         compiler_params=pltpu.CompilerParams(
             collective_id=0, has_side_effects=True, vmem_limit_bytes=60 * 1024 * 1024

time: 47.9 us -> 50.6 us (1.056)
  the two profiles are of different devices: /device:TPU:2 before, /device:TPU:1 now
where the time goes in v2:
time: 50.6 us; the launch traced here: 50.4 us
  Pallas kernels  48.9 us (97%)
  local copies, waits for them, and re-layouts  1.54 us (3%)
    pallas_call x1, Pallas kernels, shards(): pl.pallas_call(kernel, out_shape=jax.ShapeDtypeStruct((NI, 2 * LAYERS, KW...  48.9 us
    unnamed x1, local copies, waits for them, and re-layouts  1.54 us

profile of v2, /device:TPU:1, one launch (start us, length us, event | category | flops | bytes accessed | tf_op | source)
XLA Modules:
  0.0 50.4 jit_solution(9636589839453097952)
XLA Ops:
  0.0 48.9 %shard_map.55 = f32[6,32,48]{2,1,0:T(8,128)} custom-call(f32[16,768]{1,0:T(8,128)} %bitcast.8, s32[8]{0:T(128)} %lon_ref.1, s32[384]{0:T(512)} %order_ref.1, f32[3072,384]{1,0:T(8,128)} %bitcast.6, f32[3,4,4]{2,1,0:T(4,128)} %bitcast.9), custom_call_target="tpu_custom_call" | custom-call | tf_op jit(solution)/shard_map/pallas_call | solution.py:425
  48.9 1.5 %copy.7 = f32[6,48,2,16]{1,3,2,0:T(8,128)} copy(f32[6,48,2,16]{1,3,2,0:T(8,128)} %bitcast.7) | data formatting | bytes 73728

commit v3 on v2

v3 whole, which is shorter than its diff:
```python
import functools

import jax
import jax.numpy as jnp
from jax import lax
from jax.experimental import pallas as pl
from jax.experimental.pallas import tpu as pltpu
from jax.sharding import PartitionSpec as P

MESH = pl.DeviceIdType.MESH
F32 = jnp.float32
BF16 = jnp.bfloat16

MW = 384
NN = 384
NLON = 768
FIELDS = 4
LEVELS = 4
LAYERS = 16
ZH = 4
NY = 8
NX = 4
ZL = 2
R = 8
KW = 48
NI = 6
NB = 128
NA = NLON // NB
JA = 8
JB = 4

QUARTER_SIN = (6.2831854820251465, -41.34168243408203, 81.60247802734375, -76.58128356933594, 39.76072311401367)
QUARTER_COS = (0.9999999403953552, -19.739171981811523, 64.93457794189453, -85.24009704589844, 56.24053955078125)
COS = (1.0, -19.739208221435547, 64.93939208984375, -85.45665740966797, 60.242130279541016, -26.4046688079834,
       7.800131320953369, -1.4531123638153076)
SIN = (6.2831854820251465, -41.34170150756836, 81.6052474975586, -76.70580291748047, 42.05775451660156,
       -15.086565017700195, 3.7813189029693604, -0.6207788586616516)


def iota(shape, dim):
    return lax.broadcasted_iota(jnp.int32, shape, dim)


def split(x):
    hi = x.astype(BF16)
    return hi, (x - hi.astype(F32)).astype(BF16)


def nt(a, b):
    return lax.dot_general(a, b, (((1,), (1,)), ((), ())), preferred_element_type=F32)


def nn(a, b):
    return jnp.dot(a, b, preferred_element_type=F32)


def polynomial(coefficients, u):
    total = jnp.full_like(u, coefficients[-1])
    for c in coefficients[-2::-1]:
        total = total * u + c
    return total


def cos_sin(steps, points, inverse):
    turns = (steps - jnp.floor(steps * inverse + 0.5) * points) * inverse
    u = turns * turns
    return polynomial(COS, u), polynomial(SIN, u) * turns


PIECES = 4


def ring_pieces(extent):
    return [
        (direction, s, q)
        for s in range(extent // 2)
        for late in (0, 1)
        for q in range(PIECES)
        for direction in (0, 1)
        if late == (1 if (q < PIECES // 2) == (direction == 1) else 0) and s >= late
    ]


def chunk_of(extent, direction, s):
    return extent // 2 - s if direction == 0 else extent // 2 + s


def kernel(
    grid_ref, lon_ref, order_ref, leg_ref, band_ref, out_ref,
    leg_v, gv, xr, e_s, x_s, packets, arrived, picked_out, picked_in, xs, ra, rb, ring_a, ring_b, half_a, half_b,
    leg_sem, own_sem, leg_send, leg_recv, g_send, g_recv,
    ra_send, ra_recv, rb_send, rb_recv, da_send, da_recv, db_send, db_recv,
):
    lat, wave = lax.axis_index("lat"), lax.axis_index("wave")
    core = lax.rem(lat, 2)
    y = lax.rem(lat // 2, NY)
    zh = lat // (2 * NY)
    x = wave // ZL
    zl = lax.rem(wave, ZL)

    def at_y(o, c):
        return ((zh * NY + lax.rem(y + o + NY, NY)) * 2 + c, wave)

    def at_z(o, c):
        return ((lax.rem(zh + o + ZH, ZH) * NY + y) * 2 + c, wave)

    def wave_at(dx, dz):
        return lax.rem(x + dx, NX) * ZL + lax.rem(zl + dz, ZL)

    def at_w(dx, dz, dc):
        return (lat - core + lax.rem(core + dc, 2), wave_at(dx, dz))

    sibling = (lat + 1 - 2 * core, wave)
    wave_peers = [(dx, dz, dc) for dx in range(NX) for dz in range(ZL) for dc in (0, 1)][1:]
    wave_peers.sort(key=lambda to: -min(to[0], NX - to[0]) - to[1])

    leg_copies = []
    for t in range(NN // NB):
        copy = pltpu.make_async_copy(leg_ref.at[:, t * NB : (t + 1) * NB], leg_v.at[t], leg_sem.at[t])
        copy.start()
        leg_copies.append(copy)
    own_copy = pltpu.make_async_copy(grid_ref, gv, own_sem)
    own_copy.start()

    barrier = pltpu.get_barrier_semaphore()
    both = [at_w(*to) for to in wave_peers]

    def enter(others):
        for peer in both + others:
            pl.semaphore_signal(barrier, inc=1, device_id=peer, device_id_type=MESH)

    z_far, y_far = range(1, ZH), range(1, NY)

    @pl.when(core == 1)
    def _():
        others = [at_y(1, 1), at_y(-1, 1)] + [at_z(o, 1) for o in z_far] + [at_y(o, 0) for o in y_far]
        enter(others)

    @pl.when(core == 0)
    def _():
        others = [at_z(o, 1) for o in z_far] + [at_z(o, 0) for o in z_far] + [at_y(o, 0) for o in y_far]
        enter(others)

    def remote(src, dst, send, recv, peer):
        return pltpu.make_async_remote_copy(
            src_ref=src, dst_ref=dst, send_sem=send, recv_sem=recv, device_id=peer, device_id_type=MESH
        )

    sub = iota((8, NB), 0)
    rows_of = [
        (g * KW + k4 * (KW // 4), p) for g in range(8) for p in range(JA) for k4 in range(4)
    ] + [(g * KW + k4 * (KW // 4) + JA, p + JA) for g in range(8) for p in range(JB) for k4 in range(4)]
    turn_a = [lax.rem(p + JA - wave, JA) for p in range(JA)]
    turn_b = [lax.rem(p + 2 * JB - wave, JB) for p in range(JB)]
    shift = turn_a + turn_b
    waves = []
    for t in range(len(rows_of) // 8):
        column = jnp.zeros((8, NB), F32)
        for i in range(8):
            base, p = rows_of[t * 8 + i]
            column = jnp.where(sub == i, order_ref[base + shift[p]].astype(F32), column)
        waves.append(column)
    waves = jnp.concatenate(waves, axis=0)
    slots = len(rows_of)

    own_copy.wait()
    sub = iota((2 * R, NB), 0)
    points = jnp.zeros((2 * R, NB), jnp.int32)
    for r in range(R):
        points = jnp.where(sub % R == r, lon_ref[r], points)
    column = iota((2 * R, NB), 1)
    for a in range(8):
        if a < NA:
            value = jnp.where(column + a * NB < points, gv[:, a * NB : (a + 1) * NB], 0.0)
        else:
            value = jnp.zeros((2 * R, NB), F32)
        xr[pl.ds(a, 2 * R, stride=8), :] = value

    low = iota((1, NB), 1).astype(F32)
    row_of = (iota((NB, NB), 0) // 8) % R
    for r in range(R):
        inverse = 1.0 / jnp.full((1, NB), lon_ref[r], jnp.int32).astype(F32)
        u = waves * (low * inverse)
        u = u - jnp.floor(u + 0.5)
        v = jnp.abs(u) - 0.25
        square = v * v
        cosine = -v * polynomial(QUARTER_SIN, square)
        sine = polynomial(QUARTER_COS, square)
        minus_sine = jnp.where(u < 0, sine, -sine)
        for c, table in enumerate((cosine, minus_sine)):
            hi, lo = split(table)
            e_s[c * slots : (c + 1) * slots, r * 2 * NB : (r * 2 + 1) * NB] = hi
            e_s[c * slots : (c + 1) * slots, (r * 2 + 1) * NB : (r * 2 + 2) * NB] = lo
        hi, lo = split(jnp.where(row_of == r, xr[...], 0.0))
        for t in (0, 1):
            x_s[:NB, (r * 2 + t) * NB : (r * 2 + t + 1) * NB] = hi
            x_s[NB:, (r * 2 + t) * NB : (r * 2 + t + 1) * NB] = lo
    first = nt(e_s[...], x_s[...])
    first = first[:, :NB] + first[:, NB:]

    lane = iota((1, NB), 1)
    points = jnp.zeros((1, NB), jnp.int32)
    for r in range(R):
        points = jnp.where((lane // 8) % R == r, lon_ref[r], points)
    points = points.astype(F32)
    high = ((lane % 8) * NB).astype(F32)
    tw_re, tw_im = cos_sin(waves * high, points, 1.0 / points)
    factor = jnp.where(2.0 * waves < points, 1.0 / jnp.sqrt(points), 0.0)
    tw_re, tw_im = tw_re * factor, -tw_im * factor
    re, im = first[:slots], first[slots:]
    both_parts = jnp.concatenate([re * tw_re - im * tw_im, re * tw_im + im * tw_re], axis=0)
    hi, lo = split(both_parts)
    gather = jnp.where(iota((2 * R, NB), 1) // 8 == iota((2 * R, NB), 0), 1.0, 0.0).astype(BF16)
    spectrum = nt(jnp.concatenate([gather, gather], axis=1), jnp.concatenate([hi, lo], axis=1))

    part_of_a = JA * 4
    for g in range(8):
        for c_to in (0, 1):
            blocks = []
            for layer in (0, 1):
                for c in (0, 1):
                    value = spectrum[layer * R : (layer + 1) * R, c * slots : (c + 1) * slots]
                    if c_to == 1:
                        blocks.append(value[:, g * part_of_a : (g + 1) * part_of_a])
                    else:
                        start = 8 * part_of_a + g * JB * 4
                        blocks += [value[:, start : start + JB * 4]] * 2
            packets[c_to, g] = jnp.concatenate(blocks, axis=1)

    @pl.when(core == 1)
    def _():
        pl.semaphore_wait(barrier, len(both) + 2 + 2 * (ZH - 1))

    @pl.when(core == 0)
    def _():
        pl.semaphore_wait(barrier, len(both) + ZH - 1 + 2 * (NY - 1))

    def packet_copy(i):
        dx, dz, dc = wave_peers[i]
        return remote(
            packets.at[lax.rem(core + dc, 2), wave_at(dx, dz)], arrived.at[core, wave],
            g_send.at[i], g_recv.at[i], at_w(dx, dz, dc),
        )

    for i in range(len(wave_peers)):
        packet_copy(i).start()
    arrived[core, wave] = packets[core, wave]

    n_lane = iota((1, NN), 1).astype(F32) + 0.5
    z_of = jnp.floor(n_lane * (1.0 / (NI * 2 * NY)))
    rest = n_lane - z_of * (NI * 2 * NY)
    y_of = jnp.floor(rest * (1.0 / (NI * 2)))
    rest = rest - y_of * (NI * 2)
    c_of = jnp.floor(rest * (1.0 / NI))
    i_of = rest - c_of * NI - 0.5
    z_rel = z_of - zh.astype(F32)
    z_rel = jnp.where(z_rel < 0, z_rel + ZH, z_rel)
    y_rel = y_of - y.astype(F32)
    y_rel = jnp.where(y_rel < 0, y_rel + NY, y_rel)
    place_a = ((y_rel * ZH + z_rel) * 2 + c_of) * NI + i_of
    place_b = ((z_rel * NY + y_rel) * 2 + c_of) * NI + i_of
    place = jnp.where(core == 1, place_a, place_b)

    def slot(g, q):
        return (q % 4) * (KW // 4) + 2 * g + q // 4

    groups = KW // 8
    cut = JA // 2
    near, far = cut * 8, (groups - cut) * 8
    for copy in leg_copies:
        copy.wait()
    n_of = iota((R, NN), 1)

    def pick(g, q):
        m = order_ref[wave * KW + slot(g, q)]
        picked = jnp.concatenate([leg_v[t, pl.ds(m, R, stride=MW), :] for t in range(NN // NB)], axis=1)
        return jnp.where(n_of >= m, picked, 0.0)

    def rows_copy(c_from):
        count = far if c_from == 1 else near
        return remote(
            picked_out.at[pl.ds(0, count)], picked_in.at[pl.ds(0, count), c_from], leg_send, leg_recv, sibling
        )

    @pl.when(core == 1)
    def _():
        for at in range(far):
            picked_out[at] = pick(cut + at // 8, at % 8)
        rows_copy(1).start()
        for at in range(near):
            picked_in[at, 1] = pick(at // 8, at % 8)

    @pl.when(core == 0)
    def _():
        for at in range(near):
            picked_out[at] = pick(at // 8, at % 8)
        rows_copy(0).start()
        for at in range(far):
            picked_in[at, 0] = pick(cut + at // 8, at % 8)

    order = jnp.where(iota((NN, NN), 0).astype(F32) == place, 1.0, 0.0).astype(BF16)

    def turn_rows(count):
        for g in range(count // 8):
            hi, lo = split(picked_in[g * 8 : (g + 1) * 8].reshape(8 * 2 * R, NN))
            xs[g] = nt(order, jnp.concatenate([hi, lo], axis=0)).astype(BF16)

    lanes = iota((2 * R, NB), 1)
    k4_of = lanes % 4
    place_of = (lanes // 4) % 8
    per_core = 2 * R

    def values_of(j):
        total = jnp.zeros((per_core, NB), F32)
        for g in range(8):
            value = jnp.concatenate([arrived[0, g], arrived[1, g]], axis=0)
            total = jnp.where(place_of == (j + g) % 8, value, total)
        if j == 0:
            return total
        near_roll = pltpu.roll(total, NB - 4 * j, 1)
        far_roll = pltpu.roll(total, 32 - 4 * j, 1)
        return jnp.where(place_of + j < 8, near_roll, far_roll)

    def partial_sums(count, target, width):
        for g in range(count):
            rows = []
            zero = jnp.zeros((per_core, NB), F32)
            for t in (0, 1):
                value = values_of(2 * g + t)
                for k4 in range(4):
                    one = jnp.where(k4_of == k4, value, 0.0)
                    rows.append(jnp.concatenate([zero, one] if t else [one, zero], axis=1))
            hi, lo = split(jnp.concatenate(rows, axis=0))
            turned = xs[g]
            sums = nn(turned, jnp.concatenate([hi, hi], axis=0)) + nn(turned[:, :NB], lo)
            for t in (0, 1):
                target[pl.ds(2 * g + t, NN, stride=width), :] = sums[:, t * NB : (t + 1) * NB]

    part_a = NN // NY * JA
    part_b = NN // ZH * JB
    rows_a, rows_b = NI * JA, NI * JB
    y_order = sorted(range(NY), key=lambda o: -min(o, NY - o))
    z_order = sorted(range(ZH), key=lambda o: -min(o, ZH - o))
    def piece_rows(part, o, q):
        return pl.ds(o * part + q * (part // PIECES), part // PIECES)

    def ring_a_copy(direction, s, q):
        return remote(
            ra.at[piece_rows(part_a, chunk_of(NY, direction, s), q)], ring_a.at[direction, s, q],
            ra_send.at[direction, s, q], ra_recv.at[direction, s, q], at_y(1 - 2 * direction, 1),
        )

    def ring_b_copy(direction, s, q):
        return remote(
            rb.at[piece_rows(part_b, chunk_of(ZH, direction, s), q)], ring_b.at[direction, s, q],
            rb_send.at[direction, s, q], rb_recv.at[direction, s, q], at_z(1 - 2 * direction, 0),
        )

    def reduce_ring(extent, part, own, landing, copy, finish):
        every = ring_pieces(extent)

        first = [p for p in every if (p[0], p[1] - 1, p[2]) not in every]
        for p in first + [p for p in every if p not in first]:
            direction, s, q = p
            o = chunk_of(extent, direction, s)
            if p not in first:
                rows = piece_rows(part, o, q)
                copy(direction, s - 1, q).wait_recv()
                own[rows, :] = own[rows, :] + landing[direction, s - 1, q]
            copy(*p).start()
        last = extent // 2 - 1
        for q in range(PIECES):
            rows = piece_rows(part, 0, q)
            total = own[rows, :]
            for direction in (0, 1):
                if (direction, last, q) in every:
                    copy(direction, last, q).wait_recv()
                    total = total + landing[direction, last, q]
            own[rows, :] = total
            finish(q)

    def end_a_copy(o, c):
        return remote(
            ra.at[pl.ds((o * 2 + c) * rows_a, rows_a)], half_a.at[pl.ds(o * rows_a, rows_a)],
            da_send.at[o, c], da_recv.at[o], at_z(o, c) if o else sibling,
        )

    def end_b_copy(o, c):
        return remote(
            rb.at[pl.ds((o * 2 + c) * rows_b, rows_b)], half_b.at[pl.ds(o * rows_b, rows_b)],
            db_send.at[o, c], db_recv.at[o], at_y(o, c) if o else sibling,
        )

    end_a = [(o, c) for o in z_order for c in (0, 1) if (o, c) != (0, 1)]
    end_b = [(o, c) for o in y_order for c in (0, 1) if (o, c) != (0, 0)]

    @pl.when(core == 1)
    def _():
        rows_copy(0).wait_recv()
        turn_rows(near)
        for i in range(len(wave_peers)):
            packet_copy(i).wait_recv()
        partial_sums(cut, ra, JA)

        def finish(q):
            for o, c in end_a:
                if (o * 2 + c) * rows_a // (part_a // PIECES) == q:
                    end_a_copy(o, c).start()

        reduce_ring(NY, part_a, ra, ring_a, ring_a_copy, finish)
        half_a[:rows_a, :] = ra[rows_a : 2 * rows_a, :]
        end_b_copy(0, 1).wait_recv()

    @pl.when(core == 0)
    def _():
        rows_copy(1).wait_recv()
        turn_rows(far)
        for i in range(len(wave_peers)):
            packet_copy(i).wait_recv()
        partial_sums(groups - cut, rb, JB)

        def finish(q):
            for o, c in end_b:
                if (o * 2 + c) * rows_b // (part_b // PIECES) == q:
                    end_b_copy(o, c).start()

        reduce_ring(ZH, part_b, rb, ring_b, ring_b_copy, finish)
        half_b[:rows_b, :] = rb[:rows_b, :]
        end_a_copy(0, 0).wait_recv()

    band = [jnp.zeros((1, NB), F32) for _ in range(3)]
    lane = iota((1, NB), 1)
    odd = lane // (NB // 2)
    layer_of = 2 * ((lane // 4) % 8) + odd
    for d in range(3):
        for f in range(FIELDS):
            for l in range(LEVELS):
                if (d, l) in ((0, 0), (2, LEVELS - 1)):
                    continue
                band[d] = jnp.where(layer_of == f * LEVELS + l, band_ref[d, f, l], band[d])

    def vertical(total, width):
        degree = iota(total.shape, 0) // width + lat * NI
        degree = degree.astype(F32)
        ratio = degree * (degree + 1.0) * (1.0 / (MW * MW))
        other = pltpu.roll(total, NB // 2, 1)
        below = jnp.where(odd == 1, other, pltpu.roll(total, NB // 2 + 4, 1))
        above = jnp.where(odd == 0, other, pltpu.roll(total, NB // 2 - 4, 1))
        return total + ratio * (band[0] * below + band[1] * total + band[2] * above)

    total_b = half_b[:rows_b, :]
    for o in y_far:
        end_b_copy(o, 0).wait_recv()
        total_b = total_b + half_b[o * rows_b : (o + 1) * rows_b, :]
    total_b = vertical(total_b, JB)
    total_a = half_a[:rows_a, :]
    for o in z_far:
        end_a_copy(o, 0).wait_recv()
        total_a = total_a + half_a[o * rows_a : (o + 1) * rows_a, :]
    total_a = vertical(total_a, JA)

    total = jnp.concatenate([total_a, total_b], axis=0)
    hi, lo = split(total)
    rest = (total - hi.astype(F32) - lo.astype(F32)).astype(BF16)
    row, lane = iota((NB, NB), 0), iota((NB, NB), 1)
    cl = 2 * LAYERS
    source = (row % 2) * 64 + ((row % cl) // LAYERS) * 32 + ((row % LAYERS) // 2) * 4 + row // cl
    chosen = jnp.where(lane == source, 1.0, 0.0).astype(BF16)
    turned = nt(jnp.concatenate([chosen] * 3, axis=1), jnp.concatenate([hi, lo, rest], axis=1))
    for i in range(NI):
        pieces = []
        for k4 in range(4):
            rows = turned[k4 * cl : (k4 + 1) * cl]
            pieces.append(rows[:, i * JA : (i + 1) * JA])
            pieces.append(rows[:, rows_a + i * JB : rows_a + (i + 1) * JB])
        out_ref[i] = jnp.concatenate(pieces, axis=1)

    for i in range(len(wave_peers)):
        packet_copy(i).wait_send()

    @pl.when(core == 1)
    def _():
        rows_copy(1).wait_send()
        for p in ring_pieces(NY):
            ring_a_copy(*p).wait_send()
        for o, c in end_a:
            end_a_copy(o, c).wait_send()

    @pl.when(core == 0)
    def _():
        rows_copy(0).wait_send()
        for p in ring_pieces(ZH):
            ring_b_copy(*p).wait_send()
        for o, c in end_b:
            end_b_copy(o, c).wait_send()


def shards(grid_field, row_longitudes, owner_order, legendre, vertical_band):
    lw = grid_field.shape[0]
    dma = pltpu.SemaphoreType.DMA
    vmem = pltpu.VMEM
    smem = pl.BlockSpec(memory_space=pltpu.SMEM)
    hbm = pl.BlockSpec(memory_space=pltpu.HBM)
    part_a, part_b = NN // NY * JA, NN // ZH * JB
    out = pl.pallas_call(
        kernel,
        out_shape=jax.ShapeDtypeStruct((NI, 2 * LAYERS, KW), F32),
        in_specs=[hbm, smem, smem, hbm, smem],
        out_specs=pl.BlockSpec(memory_space=pltpu.VMEM),
        scratch_shapes=[
            vmem((NN // NB, R * MW, NB), F32),
            vmem((2 * R, NLON), F32),
            vmem((NB, NB), F32),
            vmem((2 * MW, R * 2 * NB), BF16),
            vmem((2 * NB, R * 2 * NB), BF16),
            vmem((2, 8, R, NB), F32),
            vmem((2, 8, R, NB), F32),
            vmem((JA * 4, R, NN), F32),
            vmem((JA * 4, 2, R, NN), F32),
            vmem((JA // 2, NN, 2 * NB), BF16),
            vmem((NN * JA, NB), F32),
            vmem((NN * JB, NB), F32),
            vmem((2, NY // 2, PIECES, part_a // PIECES, NB), F32),
            vmem((2, ZH // 2, PIECES, part_b // PIECES, NB), F32),
            vmem((ZH * NI * JA, NB), F32),
            vmem((NY * NI * JB, NB), F32),
            dma((NN // NB,)), dma, dma, dma,
            dma((2 * NX * ZL - 1,)), dma((2 * NX * ZL - 1,)),
            dma((2, NY // 2, PIECES)), dma((2, NY // 2, PIECES)),
            dma((2, ZH // 2, PIECES)), dma((2, ZH // 2, PIECES)),
            dma((ZH, 2)), dma((ZH,)), dma((NY, 2)), dma((NY,)),
        ],
        compiler_params=pltpu.CompilerParams(
            collective_id=0, has_side_effects=True, vmem_limit_bytes=60 * 1024 * 1024
        ),
    )(
        grid_field.reshape(lw * R, NLON), row_longitudes, owner_order, legendre.reshape(R * MW, NN),
        vertical_band.transpose(1, 0, 2),
    )
    return out.reshape(NI, 2, LAYERS, KW).transpose(0, 3, 1, 2)


def solution(mesh):
    placed = (P("wave", "lat", None), P("lat"), P(), P("lat", None, None), P())
    return jax.shard_map(
        shards, mesh=mesh, in_specs=placed, out_specs=P("lat", "wave", None, None), check_vma=False
    )
```

time: 50.6 us -> 46.9 us (0.927)
  Pallas kernels: 48.9 us -> 45.1 us
    pallas_call x1, Pallas kernels: 48.9 us -> 45.1 us  [shards(): pl.pallas_call(kernel, out_shape=jax.ShapeDtypeStruct((NI, 2 * LAYERS, KW...]
where the time goes in v3:
time: 46.9 us; the launch traced here: 46.7 us
  Pallas kernels  45.1 us (96%)
  local copies, waits for them, and re-layouts  1.54 us (3%)
    pallas_call x1, Pallas kernels, shards(): pl.pallas_call(kernel, out_shape=jax.ShapeDtypeStruct((NI, 2 * LAYERS, KW...  45.1 us
    unnamed x1, local copies, waits for them, and re-layouts  1.54 us

profile of v3, /device:TPU:1, one launch (start us, length us, event | category | flops | bytes accessed | tf_op | source)
XLA Modules:
  0.0 46.7 jit_solution(16968726665177683187)
XLA Ops:
  0.0 45.1 %shard_map.55 = f32[6,32,48]{2,1,0:T(8,128)} custom-call(f32[16,768]{1,0:T(8,128)} %bitcast.8, s32[8]{0:T(128)} %lon_ref.1, s32[384]{0:T(512)} %order_ref.1, f32[3072,384]{1,0:T(8,128)} %bitcast.6, f32[3,4,4]{2,1,0:T(4,128)} %bitcast.9), custom_call_target="tpu_custom_call" | custom-call | tf_op jit(solution)/shard_map/pallas_call | solution.py:505
  45.2 1.5 %copy.7 = f32[6,48,2,16]{1,3,2,0:T(8,128)} copy(f32[6,48,2,16]{1,3,2,0:T(8,128)} %bitcast.7) | data formatting | bytes 73728

commit v4 on v3

--- a/solution.py
+++ b/solution.py
@@ -86,9 +86,9 @@
 
 
 def kernel(
-    grid_ref, lon_ref, order_ref, leg_ref, band_ref, out_ref,
-    leg_v, gv, xr, e_s, x_s, packets, arrived, picked_out, picked_in, xs, ra, rb, ring_a, ring_b, half_a, half_b,
-    leg_sem, own_sem, leg_send, leg_recv, g_send, g_recv,
+    grid_ref, lon_in, order_in, leg_ref, band_in, out_ref,
+    lon_ref, order_ref, band_ref, order_row, leg_v, gv, xr, packets, arrived, picked_out, picked_in, xs, fd, ra, rb, ring_a, ring_b, half_a, half_b,
+    small_sem, leg_sem, own_sem, leg_send, leg_recv, g_send, g_recv,
     ra_send, ra_recv, rb_send, rb_recv, da_send, da_recv, db_send, db_recv,
 ):
     lat, wave = lax.axis_index("lat"), lax.axis_index("wave")
@@ -114,14 +114,21 @@
     wave_peers = [(dx, dz, dc) for dx in range(NX) for dz in range(ZL) for dc in (0, 1)][1:]
     wave_peers.sort(key=lambda to: -min(to[0], NX - to[0]) - to[1])
 
+    small = [
+        pltpu.make_async_copy(source, target, small_sem.at[i])
+        for i, (source, target) in enumerate(
+            ((lon_in, lon_ref), (order_in, order_row), (order_in, order_ref), (band_in, band_ref))
+        )
+    ]
+    for copy in small:
+        copy.start()
+    own_copy = pltpu.make_async_copy(grid_ref, gv, own_sem)
+    own_copy.start()
     leg_copies = []
     for t in range(NN // NB):
         copy = pltpu.make_async_copy(leg_ref.at[:, t * NB : (t + 1) * NB], leg_v.at[t], leg_sem.at[t])
         copy.start()
         leg_copies.append(copy)
-    own_copy = pltpu.make_async_copy(grid_ref, gv, own_sem)
-    own_copy.start()
-
     barrier = pltpu.get_barrier_semaphore()
     both = [at_w(*to) for to in wave_peers]
 
@@ -146,22 +153,22 @@
             src_ref=src, dst_ref=dst, send_sem=send, recv_sem=recv, device_id=peer, device_id_type=MESH
         )
 
-    sub = iota((8, NB), 0)
-    rows_of = [
-        (g * KW + k4 * (KW // 4), p) for g in range(8) for p in range(JA) for k4 in range(4)
-    ] + [(g * KW + k4 * (KW // 4) + JA, p + JA) for g in range(8) for p in range(JB) for k4 in range(4)]
-    turn_a = [lax.rem(p + JA - wave, JA) for p in range(JA)]
-    turn_b = [lax.rem(p + 2 * JB - wave, JB) for p in range(JB)]
-    shift = turn_a + turn_b
-    waves = []
-    for t in range(len(rows_of) // 8):
-        column = jnp.zeros((8, NB), F32)
-        for i in range(8):
-            base, p = rows_of[t * 8 + i]
-            column = jnp.where(sub == i, order_ref[base + shift[p]].astype(F32), column)
-        waves.append(column)
-    waves = jnp.concatenate(waves, axis=0)
-    slots = len(rows_of)
+    small[0].wait()
+    small[1].wait()
+    slots = MW
+    rows_a_all = 8 * JA * 4
+    row = iota((slots, NB), 0)
+    in_a = row < rows_a_all
+    rest = jnp.where(in_a, row, row - rows_a_all)
+    place = (rest // 4) + 8 - wave
+    wave_of = jnp.where(in_a, rest // (JA * 4), rest // (JB * 4))
+    j_of = jnp.where(in_a, place % JA, JA + place % JB)
+    slot_of = wave_of * KW + (rest % 4) * (KW // 4) + j_of
+    hit = jnp.concatenate(
+        [jnp.where(slot_of == iota((slots, NB), 1) + t * NB, 1.0, 0.0).astype(BF16) for t in range(MW // NB)], axis=1
+    )
+    hi, lo = split(jnp.broadcast_to(order_row[...].astype(F32)[None, :], (NB, MW)))
+    waves = nt(jnp.concatenate([hit, hit], axis=1), jnp.concatenate([hi, lo], axis=1))
 
     own_copy.wait()
     sub = iota((2 * R, NB), 0)
@@ -178,6 +185,7 @@
 
     low = iota((1, NB), 1).astype(F32)
     row_of = (iota((NB, NB), 0) // 8) % R
+    first = [None, None]
     for r in range(R):
         inverse = 1.0 / jnp.full((1, NB), lon_ref[r], jnp.int32).astype(F32)
         u = waves * (low * inverse)
@@ -187,16 +195,12 @@
         cosine = -v * polynomial(QUARTER_SIN, square)
         sine = polynomial(QUARTER_COS, square)
         minus_sine = jnp.where(u < 0, sine, -sine)
+        hi, lo = split(jnp.where(row_of == r, xr[...], 0.0))
+        columns = jnp.concatenate([jnp.concatenate([hi, hi], axis=1), jnp.concatenate([lo, lo], axis=1)], axis=0)
         for c, table in enumerate((cosine, minus_sine)):
-            hi, lo = split(table)
-            e_s[c * slots : (c + 1) * slots, r * 2 * NB : (r * 2 + 1) * NB] = hi
-            e_s[c * slots : (c + 1) * slots, (r * 2 + 1) * NB : (r * 2 + 2) * NB] = lo
-        hi, lo = split(jnp.where(row_of == r, xr[...], 0.0))
-        for t in (0, 1):
-            x_s[:NB, (r * 2 + t) * NB : (r * 2 + t + 1) * NB] = hi
-            x_s[NB:, (r * 2 + t) * NB : (r * 2 + t + 1) * NB] = lo
-    first = nt(e_s[...], x_s[...])
-    first = first[:, :NB] + first[:, NB:]
+            part = nt(jnp.concatenate(split(table), axis=1), columns)
+            part = part[:, :NB] + part[:, NB:]
+            first[c] = part if r == 0 else first[c] + part
 
     lane = iota((1, NB), 1)
     points = jnp.zeros((1, NB), jnp.int32)
@@ -207,7 +211,7 @@
     tw_re, tw_im = cos_sin(waves * high, points, 1.0 / points)
     factor = jnp.where(2.0 * waves < points, 1.0 / jnp.sqrt(points), 0.0)
     tw_re, tw_im = tw_re * factor, -tw_im * factor
-    re, im = first[:slots], first[slots:]
+    re, im = first
     both_parts = jnp.concatenate([re * tw_re - im * tw_im, re * tw_im + im * tw_re], axis=0)
     hi, lo = split(both_parts)
     gather = jnp.where(iota((2 * R, NB), 1) // 8 == iota((2 * R, NB), 0), 1.0, 0.0).astype(BF16)
@@ -267,6 +271,7 @@
     groups = KW // 8
     cut = JA // 2
     near, far = cut * 8, (groups - cut) * 8
+    small[2].wait()
     for copy in leg_copies:
         copy.wait()
     n_of = iota((R, NN), 1)
@@ -321,7 +326,7 @@
         far_roll = pltpu.roll(total, 32 - 4 * j, 1)
         return jnp.where(place_of + j < 8, near_roll, far_roll)
 
-    def partial_sums(count, target, width):
+    def diagonals(count):
         for g in range(count):
             rows = []
             zero = jnp.zeros((per_core, NB), F32)
@@ -331,10 +336,15 @@
                     one = jnp.where(k4_of == k4, value, 0.0)
                     rows.append(jnp.concatenate([zero, one] if t else [one, zero], axis=1))
             hi, lo = split(jnp.concatenate(rows, axis=0))
-            turned = xs[g]
-            sums = nn(turned, jnp.concatenate([hi, hi], axis=0)) + nn(turned[:, :NB], lo)
+            fd[g] = jnp.concatenate([hi, hi, lo], axis=0)
+
+    def chunk_sums(o, count, extent, target, width):
+        rows = NN // extent
+        for g in range(count):
+            turned = xs[g, o * rows : (o + 1) * rows, :]
+            sums = nn(turned, fd[g, : 2 * NB, :]) + nn(turned[:, :NB], fd[g, 2 * NB :, :])
             for t in (0, 1):
-                target[pl.ds(2 * g + t, NN, stride=width), :] = sums[:, t * NB : (t + 1) * NB]
+                target[pl.ds(o * rows * width + 2 * g + t, rows, stride=width), :] = sums[:, t * NB : (t + 1) * NB]
 
     part_a = NN // NY * JA
     part_b = NN // ZH * JB
@@ -356,18 +366,22 @@
             rb_send.at[direction, s, q], rb_recv.at[direction, s, q], at_z(1 - 2 * direction, 0),
         )
 
-    def reduce_ring(extent, part, own, landing, copy, finish):
+    def reduce_ring(extent, part, own, landing, copy, sums, finish):
         every = ring_pieces(extent)
 
         first = [p for p in every if (p[0], p[1] - 1, p[2]) not in every]
-        for p in first + [p for p in every if p not in first]:
-            direction, s, q = p
-            o = chunk_of(extent, direction, s)
+        for o in sorted(range(extent), key=lambda o: -min(o, extent - o)):
+            sums(o)
+            for p in first:
+                if chunk_of(extent, p[0], p[1]) == o:
+                    copy(*p).start()
+        for p in every:
             if p not in first:
-                rows = piece_rows(part, o, q)
+                direction, s, q = p
+                rows = piece_rows(part, chunk_of(extent, direction, s), q)
                 copy(direction, s - 1, q).wait_recv()
                 own[rows, :] = own[rows, :] + landing[direction, s - 1, q]
-            copy(*p).start()
+                copy(*p).start()
         last = extent // 2 - 1
         for q in range(PIECES):
             rows = piece_rows(part, 0, q)
@@ -400,14 +414,14 @@
         turn_rows(near)
         for i in range(len(wave_peers)):
             packet_copy(i).wait_recv()
-        partial_sums(cut, ra, JA)
+        diagonals(cut)
 
         def finish(q):
             for o, c in end_a:
                 if (o * 2 + c) * rows_a // (part_a // PIECES) == q:
                     end_a_copy(o, c).start()
 
-        reduce_ring(NY, part_a, ra, ring_a, ring_a_copy, finish)
+        reduce_ring(NY, part_a, ra, ring_a, ring_a_copy, lambda o: chunk_sums(o, cut, NY, ra, JA), finish)
         half_a[:rows_a, :] = ra[rows_a : 2 * rows_a, :]
         end_b_copy(0, 1).wait_recv()
 
@@ -417,17 +431,18 @@
         turn_rows(far)
         for i in range(len(wave_peers)):
             packet_copy(i).wait_recv()
-        partial_sums(groups - cut, rb, JB)
+        diagonals(groups - cut)
 
         def finish(q):
             for o, c in end_b:
                 if (o * 2 + c) * rows_b // (part_b // PIECES) == q:
                     end_b_copy(o, c).start()
 
-        reduce_ring(ZH, part_b, rb, ring_b, ring_b_copy, finish)
+        reduce_ring(ZH, part_b, rb, ring_b, ring_b_copy, lambda o: chunk_sums(o, groups - cut, ZH, rb, JB), finish)
         half_b[:rows_b, :] = rb[:rows_b, :]
         end_a_copy(0, 0).wait_recv()
 
+    small[3].wait()
     band = [jnp.zeros((1, NB), F32) for _ in range(3)]
     lane = iota((1, NB), 1)
     odd = lane // (NB // 2)
@@ -499,32 +514,35 @@
     lw = grid_field.shape[0]
     dma = pltpu.SemaphoreType.DMA
     vmem = pltpu.VMEM
-    smem = pl.BlockSpec(memory_space=pltpu.SMEM)
+    smem = pltpu.SMEM
     hbm = pl.BlockSpec(memory_space=pltpu.HBM)
     part_a, part_b = NN // NY * JA, NN // ZH * JB
     out = pl.pallas_call(
         kernel,
         out_shape=jax.ShapeDtypeStruct((NI, 2 * LAYERS, KW), F32),
-        in_specs=[hbm, smem, smem, hbm, smem],
+        in_specs=[hbm] * 5,
         out_specs=pl.BlockSpec(memory_space=pltpu.VMEM),
         scratch_shapes=[
+            smem((R,), jnp.int32),
+            smem((MW,), jnp.int32),
+            smem((3, FIELDS, LEVELS), F32),
+            vmem((MW,), jnp.int32),
             vmem((NN // NB, R * MW, NB), F32),
             vmem((2 * R, NLON), F32),
             vmem((NB, NB), F32),
-            vmem((2 * MW, R * 2 * NB), BF16),
-            vmem((2 * NB, R * 2 * NB), BF16),
             vmem((2, 8, R, NB), F32),
             vmem((2, 8, R, NB), F32),
             vmem((JA * 4, R, NN), F32),
             vmem((JA * 4, 2, R, NN), F32),
             vmem((JA // 2, NN, 2 * NB), BF16),
+            vmem((JA // 2, 3 * NB, 2 * NB), BF16),
             vmem((NN * JA, NB), F32),
             vmem((NN * JB, NB), F32),
             vmem((2, NY // 2, PIECES, part_a // PIECES, NB), F32),
             vmem((2, ZH // 2, PIECES, part_b // PIECES, NB), F32),
             vmem((ZH * NI * JA, NB), F32),
             vmem((NY * NI * JB, NB), F32),
-            dma((NN // NB,)), dma, dma, dma,
+            dma((4,)), dma((NN // NB,)), dma, dma, dma,
             dma((2 * NX * ZL - 1,)), dma((2 * NX * ZL - 1,)),
             dma((2, NY // 2, PIECES)), dma((2, NY // 2, PIECES)),
             dma((2, ZH // 2, PIECES)), dma((2, ZH // 2, PIECES)),

time: 46.9 us -> 45.1 us (0.962)
  Pallas kernels: 45.1 us -> 43.4 us
    pallas_call x1, Pallas kernels: 45.1 us -> 43.4 us  [shards(): pl.pallas_call(kernel, out_shape=jax.ShapeDtypeStruct((NI, 2 * LAYERS, KW...]
where the time goes in v4:
time: 45.1 us; the launch traced here: 44.9 us
  Pallas kernels  43.4 us (96%)
  local copies, waits for them, and re-layouts  1.54 us (3%)
    pallas_call x1, Pallas kernels, shards(): pl.pallas_call(kernel, out_shape=jax.ShapeDtypeStruct((NI, 2 * LAYERS, KW...  43.4 us
    unnamed x1, local copies, waits for them, and re-layouts  1.54 us

profile of v4, /device:TPU:1, one launch (start us, length us, event | category | flops | bytes accessed | tf_op | source)
XLA Modules:
  0.0 44.9 jit_solution(1272191862726629973)
XLA Ops:
  0.0 43.4 %shard_map.55 = f32[6,32,48]{2,1,0:T(8,128)} custom-call(f32[16,768]{1,0:T(8,128)} %bitcast.8, s32[8]{0:T(128)} %lon_in.1, s32[384]{0:T(512)} %order_in.1, f32[3072,384]{1,0:T(8,128)} %bitcast.6, f32[3,4,4]{2,1,0:T(4,128)} %bitcast.9), custom_call_target="tpu_custom_call" | custom-call | tf_op jit(solution)/shard_map/pallas_call | solution.py:520
  43.4 1.5 %copy.7 = f32[6,48,2,16]{1,3,2,0:T(8,128)} copy(f32[6,48,2,16]{1,3,2,0:T(8,128)} %bitcast.7) | data formatting | bytes 73728

commit v5 on v4

--- a/solution.py
+++ b/solution.py
@@ -375,15 +375,15 @@
             for p in first:
                 if chunk_of(extent, p[0], p[1]) == o:
                     copy(*p).start()
-        for p in every:
-            if p not in first:
-                direction, s, q = p
-                rows = piece_rows(part, chunk_of(extent, direction, s), q)
-                copy(direction, s - 1, q).wait_recv()
-                own[rows, :] = own[rows, :] + landing[direction, s - 1, q]
-                copy(*p).start()
+        start = {(direction, q): s for direction, s, q in first}
+        moved = [p for p in every if p not in first]
+        for direction, s, q in sorted(moved, key=lambda p: p[1] - start[p[0], p[2]]):
+            rows = piece_rows(part, chunk_of(extent, direction, s), q)
+            copy(direction, s - 1, q).wait_recv()
+            own[rows, :] = own[rows, :] + landing[direction, s - 1, q]
+            copy(direction, s, q).start()
         last = extent // 2 - 1
-        for q in range(PIECES):
+        for q in sorted(range(PIECES), key=lambda q: abs(2 * q - PIECES)):
             rows = piece_rows(part, 0, q)
             total = own[rows, :]
             for direction in (0, 1):

time: 45.1 us -> 41.3 us (0.916)
  Pallas kernels: 43.4 us -> 39.6 us
    pallas_call x1, Pallas kernels: 43.4 us -> 39.6 us  [shards(): pl.pallas_call(kernel, out_shape=jax.ShapeDtypeStruct((NI, 2 * LAYERS, KW...]
where the time goes in v5:
time: 41.3 us; the launch traced here: 41.1 us
  Pallas kernels  39.6 us (96%)
  local copies, waits for them, and re-layouts  1.54 us (4%)
    pallas_call x1, Pallas kernels, shards(): pl.pallas_call(kernel, out_shape=jax.ShapeDtypeStruct((NI, 2 * LAYERS, KW...  39.6 us
    unnamed x1, local copies, waits for them, and re-layouts  1.54 us

profile of v5, /device:TPU:1, one launch (start us, length us, event | category | flops | bytes accessed | tf_op | source)
XLA Modules:
  0.0 41.1 jit_solution(11843956305348352865)
XLA Ops:
  0.0 39.6 %shard_map.55 = f32[6,32,48]{2,1,0:T(8,128)} custom-call(f32[16,768]{1,0:T(8,128)} %bitcast.8, s32[8]{0:T(128)} %lon_in.1, s32[384]{0:T(512)} %order_in.1, f32[3072,384]{1,0:T(8,128)} %bitcast.6, f32[3,4,4]{2,1,0:T(4,128)} %bitcast.9), custom_call_target="tpu_custom_call" | custom-call | tf_op jit(solution)/shard_map/pallas_call | solution.py:520
  39.6 1.5 %copy.7 = f32[6,48,2,16]{1,3,2,0:T(8,128)} copy(f32[6,48,2,16]{1,3,2,0:T(8,128)} %bitcast.7) | data formatting | bytes 73728

commit v6 on v5

--- a/solution.py
+++ b/solution.py
@@ -405,43 +405,6 @@
             db_send.at[o, c], db_recv.at[o], at_y(o, c) if o else sibling,
         )
 
-    end_a = [(o, c) for o in z_order for c in (0, 1) if (o, c) != (0, 1)]
-    end_b = [(o, c) for o in y_order for c in (0, 1) if (o, c) != (0, 0)]
-
-    @pl.when(core == 1)
-    def _():
-        rows_copy(0).wait_recv()
-        turn_rows(near)
-        for i in range(len(wave_peers)):
-            packet_copy(i).wait_recv()
-        diagonals(cut)
-
-        def finish(q):
-            for o, c in end_a:
-                if (o * 2 + c) * rows_a // (part_a // PIECES) == q:
-                    end_a_copy(o, c).start()
-
-        reduce_ring(NY, part_a, ra, ring_a, ring_a_copy, lambda o: chunk_sums(o, cut, NY, ra, JA), finish)
-        half_a[:rows_a, :] = ra[rows_a : 2 * rows_a, :]
-        end_b_copy(0, 1).wait_recv()
-
-    @pl.when(core == 0)
-    def _():
-        rows_copy(1).wait_recv()
-        turn_rows(far)
-        for i in range(len(wave_peers)):
-            packet_copy(i).wait_recv()
-        diagonals(groups - cut)
-
-        def finish(q):
-            for o, c in end_b:
-                if (o * 2 + c) * rows_b // (part_b // PIECES) == q:
-                    end_b_copy(o, c).start()
-
-        reduce_ring(ZH, part_b, rb, ring_b, ring_b_copy, lambda o: chunk_sums(o, groups - cut, ZH, rb, JB), finish)
-        half_b[:rows_b, :] = rb[:rows_b, :]
-        end_a_copy(0, 0).wait_recv()
-
     small[3].wait()
     band = [jnp.zeros((1, NB), F32) for _ in range(3)]
     lane = iota((1, NB), 1)
@@ -454,6 +417,48 @@
                     continue
                 band[d] = jnp.where(layer_of == f * LEVELS + l, band_ref[d, f, l], band[d])
 
+    row, lane_of = iota((NB, NB), 0), iota((NB, NB), 1)
+    cl = 2 * LAYERS
+    source = (row % 2) * 64 + ((row % cl) // LAYERS) * 32 + ((row % LAYERS) // 2) * 4 + row // cl
+    chosen = jnp.where(lane_of == source, 1.0, 0.0).astype(BF16)
+
+    end_a = [(o, c) for o in z_order for c in (0, 1) if (o, c) != (0, 1)]
+    end_b = [(o, c) for o in y_order for c in (0, 1) if (o, c) != (0, 0)]
+
+    @pl.when(core == 1)
+    def _():
+        rows_copy(0).wait_recv()
+        turn_rows(near)
+        for i in range(len(wave_peers)):
+            packet_copy(i).wait_recv()
+        diagonals(cut)
+
+        def finish(q):
+            for o, c in end_a:
+                if (o * 2 + c) * rows_a // (part_a // PIECES) == q:
+                    end_a_copy(o, c).start()
+
+        reduce_ring(NY, part_a, ra, ring_a, ring_a_copy, lambda o: chunk_sums(o, cut, NY, ra, JA), finish)
+        half_a[:rows_a, :] = ra[rows_a : 2 * rows_a, :]
+        end_b_copy(0, 1).wait_recv()
+
+    @pl.when(core == 0)
+    def _():
+        rows_copy(1).wait_recv()
+        turn_rows(far)
+        for i in range(len(wave_peers)):
+            packet_copy(i).wait_recv()
+        diagonals(groups - cut)
+
+        def finish(q):
+            for o, c in end_b:
+                if (o * 2 + c) * rows_b // (part_b // PIECES) == q:
+                    end_b_copy(o, c).start()
+
+        reduce_ring(ZH, part_b, rb, ring_b, ring_b_copy, lambda o: chunk_sums(o, groups - cut, ZH, rb, JB), finish)
+        half_b[:rows_b, :] = rb[:rows_b, :]
+        end_a_copy(0, 0).wait_recv()
+
     def vertical(total, width):
         degree = iota(total.shape, 0) // width + lat * NI
         degree = degree.astype(F32)
@@ -477,10 +482,6 @@
     total = jnp.concatenate([total_a, total_b], axis=0)
     hi, lo = split(total)
     rest = (total - hi.astype(F32) - lo.astype(F32)).astype(BF16)
-    row, lane = iota((NB, NB), 0), iota((NB, NB), 1)
-    cl = 2 * LAYERS
-    source = (row % 2) * 64 + ((row % cl) // LAYERS) * 32 + ((row % LAYERS) // 2) * 4 + row // cl
-    chosen = jnp.where(lane == source, 1.0, 0.0).astype(BF16)
     turned = nt(jnp.concatenate([chosen] * 3, axis=1), jnp.concatenate([hi, lo, rest], axis=1))
     for i in range(NI):
         pieces = []

time: 41.3 us -> 41.3 us (level)
  no operation moved by 1% of the time
where the time goes in v6:
time: 41.3 us; the launch traced here: 41.1 us
  Pallas kernels  39.6 us (96%)
  local copies, waits for them, and re-layouts  1.54 us (4%)
    pallas_call x1, Pallas kernels, shards(): pl.pallas_call(kernel, out_shape=jax.ShapeDtypeStruct((NI, 2 * LAYERS, KW...  39.6 us
    unnamed x1, local copies, waits for them, and re-layouts  1.54 us

profile of v6, /device:TPU:1, one launch (start us, length us, event | category | flops | bytes accessed | tf_op | source)
XLA Modules:
  0.0 41.1 jit_solution(8651230073481143545)
XLA Ops:
  0.0 39.6 %shard_map.55 = f32[6,32,48]{2,1,0:T(8,128)} custom-call(f32[16,768]{1,0:T(8,128)} %bitcast.8, s32[8]{0:T(128)} %lon_in.1, s32[384]{0:T(512)} %order_in.1, f32[3072,384]{1,0:T(8,128)} %bitcast.6, f32[3,4,4]{2,1,0:T(4,128)} %bitcast.9), custom_call_target="tpu_custom_call" | custom-call | tf_op jit(solution)/shard_map/pallas_call | solution.py:521
  39.6 1.5 %copy.7 = f32[6,48,2,16]{1,3,2,0:T(8,128)} copy(f32[6,48,2,16]{1,3,2,0:T(8,128)} %bitcast.7) | data formatting | bytes 73728
